TPU v7x, 32 devices: a whole 2x2x4 slice. The times are simulated.
32 devices in a mesh: groups: 2 (over y), dp: 4 (over z), mp: 2 (over x), sub: 2 (over core).
Axes of the slice: x: 2, y: 2, z: 4, core: 2. Of those that a mesh axis runs over, the one named last changes fastest.
Arguments:
- tokens: bfloat16 [4096, 8192], P(('groups', 'dp'), ('mp', 'sub')), parts along dimension 0, may hold values from -6 to 6
- base_weight: bfloat16 [8192, 1024], P(('mp', 'sub')), may hold values from -0.0625 to 0.0625
- tenant_down_matrix: bfloat16 [64, 8192, 64], P(('groups', 'dp'), ('mp', 'sub')), parts along dimension 0, may hold values from -0.0625 to 0.0625
- tenant_up_matrix: bfloat16 [64, 64, 1024], P(('groups', 'dp'), None, ('mp', 'sub')), parts along dimension 0, may hold values from -0.75 to 0.75
- cotangent: bfloat16 [4096, 1024], P(('groups', 'dp'), ('mp', 'sub')), parts along dimension 0, may hold values from -6 to 6
- tenant: int32 [4096, 1], P(('groups', 'dp')), parts along dimension 0, may hold values from 0 to 31; in each aligned block of 512 rows (0 to 511, 512 to 1023, ...) at most 32 rows name the same one
Outputs:
- adapted_layer_output: bfloat16 [4096, 1024], P(('groups', 'dp'), ('mp', 'sub')), parts along dimension 0
- token_grad: bfloat16 [4096, 8192], P(('groups', 'dp'), ('mp', 'sub')), parts along dimension 0
- down_gradient: float32 [64, 8192, 64], P(('groups', 'dp'), ('mp', 'sub')), parts along dimension 0
- up_gradient: float32 [64, 64, 1024], P(('groups', 'dp'), None, ('mp', 'sub')), parts along dimension 0
There are 2 independent parts, one for each index of `groups`. A program takes and returns all parts, laid end to end along the dimension named above; an argument that names none is the same for every part. Nothing has to cross between parts.
Inputs may be any that keep to these rules, and one draw needn't show every extreme that they name: The tokens of each index of dp name each tenant at most 32 times, and for every index of dp some tenant is named exactly 32 times.
All inputs are finite; a program needn't handle non-finite values.
Results may differ from a plain program's by a relative error of at most 0.004.
Values may be sent and summed in bfloat16 or wider, within the bound.
A program may use at most 128 MiB of HBM per device.

v0:
```python
import jax
import jax.numpy as jnp
from jax import lax
from jax.sharding import PartitionSpec as P

adapter_scale = 0.5


def local(tokens, base_weight, tenant_down_matrix, tenant_up_matrix, cotangent, tenant):
    tenant_groups = lax.axis_size("dp")
    resident_tenant = tenant_down_matrix.shape[0]
    rows_dev, slice_width_input = tokens.shape
    slice_width_key = cotangent.shape[1]
    slot_limit = 2 * rows_dev // (tenant_groups * resident_tenant)
    slots_count = tenant_groups * resident_tenant * slot_limit
    tenant_ids = tenant[:, 0]
    onehot = (
        tenant_ids[:, None] == jnp.arange(tenant_groups * resident_tenant, dtype=jnp.int32)[None, :]
    ).astype(jnp.int32)
    places = jnp.sum(onehot * (jnp.cumsum(onehot, axis=0) - 1), axis=1)
    target_output = tenant_ids * slot_limit + places
    columns = base_weight
    frozen_rows = lax.psum_scatter(
        lax.dot_general(
            columns, tokens, (((0,), (1,)), ((), ())), preferred_element_type=jnp.float32
        ),
        ("mp", "sub"),
        scatter_dimension=0,
        tiled=True,
    )
    columns = base_weight
    dx_base = lax.dot_general(
        lax.all_gather(cotangent, ("mp", "sub"), axis=1, tiled=True),
        columns,
        (((1,), (1,)), ((), ())),
        preferred_element_type=jnp.float32,
    )
    width_g = cotangent.shape[1]
    send_x = jnp.zeros((slots_count, slice_width_input), jnp.bfloat16).at[target_output].set(tokens)
    send_g = jnp.zeros((slots_count, width_g), jnp.bfloat16).at[target_output].set(cotangent)
    send_x = send_x.reshape(tenant_groups, resident_tenant * slot_limit, slice_width_input)
    send_g = send_g.reshape(tenant_groups, resident_tenant * slot_limit, width_g)
    recv_x, recv_g = (
        lax.all_to_all(send_x, "dp", split_axis=0, concat_axis=0, tiled=True),
        lax.all_to_all(send_g, "dp", split_axis=0, concat_axis=0, tiled=True),
    )
    recv_x = recv_x.reshape(tenant_groups, resident_tenant, slot_limit, slice_width_input)
    recv_g = recv_g.reshape(tenant_groups, resident_tenant, slot_limit, width_g)
    partial_u = jnp.einsum(
        "slcd,ldr->slcr", recv_x, tenant_down_matrix, preferred_element_type=jnp.float32
    )
    partial_v = jnp.einsum(
        "slck,lrk->slcr", recv_g, tenant_up_matrix, preferred_element_type=jnp.float32
    )
    rank_output, rank_backward = lax.psum((partial_u, partial_v), ("mp", "sub"))
    rank_output = rank_output.astype(jnp.bfloat16)
    rank_backward = rank_backward.astype(jnp.bfloat16)
    adapter_output = (
        adapter_scale
        * jnp.einsum(
            "slcr,lrk->slck", rank_output, tenant_up_matrix, preferred_element_type=jnp.float32
        )
    ).astype(jnp.bfloat16)
    adapter_input_gradient = (
        adapter_scale
        * jnp.einsum(
            "slcr,ldr->slcd", rank_backward, tenant_down_matrix, preferred_element_type=jnp.float32
        )
    ).astype(jnp.bfloat16)
    down_gradient = adapter_scale * jnp.einsum(
        "slcd,slcr->ldr", recv_x, rank_backward, preferred_element_type=jnp.float32
    )
    up_gradient = adapter_scale * jnp.einsum(
        "slcr,slck->lrk", rank_output, recv_g, preferred_element_type=jnp.float32
    )
    backward_result, back_dx = (
        lax.all_to_all(
            adapter_output.reshape(tenant_groups, resident_tenant * slot_limit, slice_width_key),
            "dp",
            split_axis=0,
            concat_axis=0,
            tiled=True,
        ),
        lax.all_to_all(
            adapter_input_gradient.reshape(
                tenant_groups, resident_tenant * slot_limit, slice_width_input
            ),
            "dp",
            split_axis=0,
            concat_axis=0,
            tiled=True,
        ),
    )
    adapter_token = backward_result.reshape(slots_count, slice_width_key)[target_output]
    token_input_gradient = back_dx.reshape(slots_count, slice_width_input)[target_output]
    adapted_layer_output = (frozen_rows.T + adapter_token.astype(jnp.float32)).astype(jnp.bfloat16)
    token_grad = (dx_base + token_input_gradient.astype(jnp.float32)).astype(jnp.bfloat16)
    return (adapted_layer_output, token_grad, down_gradient, up_gradient)


def solution(mesh):
    placed = (
        P(("groups", "dp"), ("mp", "sub")),
        P(("mp", "sub"), None),
        P(("groups", "dp"), ("mp", "sub"), None),
        P(("groups", "dp"), None, ("mp", "sub")),
        P(("groups", "dp"), ("mp", "sub")),
        P(("groups", "dp"), None),
    )
    return jax.shard_map(
        local,
        mesh=mesh,
        in_specs=placed,
        out_specs=(
            P(("groups", "dp"), ("mp", "sub")),
            P(("groups", "dp"), ("mp", "sub")),
            P(("groups", "dp"), ("mp", "sub"), None),
            P(("groups", "dp"), None, ("mp", "sub")),
        ),
        check_vma=False,
    )
```

profile of v0, /device:TPU:0, one launch (start us, length us, event | category | flops | bytes accessed | tf_op | source)
XLA Modules:
  0.0 303.9 jit_solution(777247444503939419)
XLA Ops:
  7.2 0.0 copy-start
  7.2 0.8 fusion.27
  8.0 1.2 reduce-window.6
  9.2 0.2 slice_reduce_fusion
  9.4 0.8 fusion.26
  10.2 0.7 compare_select_fusion
  10.9 3.5 %scatter_custom_fusion.1 = bf16[1024,256]{1,0:T(8,128)(2,1)} fusion(s32[512]{0:T(512)S(1)} %bitcast.78, bf16[512,256]{1,0:T(8,128)(2,1)} %param.10, bf16[]{:T(256)} %constant.6.clone.1), kind=kCustom, calls=%fused_computation.28 | custom fusion | bytes 524800 | tf_op jit(solution)/shard_map/scatter | solution.py:40
  14.5 6.3 %all-to-all-start.2 = ((bf16[4,256,256]{2,1,0:T(8,128)(2,1)}), bf16[4,256,256]{2,1,0:T(8,128)(2,1)S(1)}, u32[]{:S(2)}, u32[]{:S(2)}) async-start(bf16[4,256,256]{2,1,0:T(8,128)(2,1)} %bitcast.16), calls=%async_computation.3 | async-start | bytes 1048576 | tf_op jit(solution)/shard_map/all_to_all | solution.py:45
  20.8 7.3 %scatter_custom_fusion = bf16[1024,2048]{1,0:T(8,128)(2,1)} fusion(s32[512]{0:T(512)S(1)} %bitcast.79, bf16[512,2048]{1,0:T(8,128)(2,1)} %param.6, bf16[]{:T(256)} %constant.6.clone.1), kind=kCustom, calls=%fused_computation.12 | custom fusion | bytes 4194816 | tf_op jit(solution)/shard_map/scatter | solution.py:39
  28.1 7.2 %all-to-all-done.2 = bf16[4,256,256]{2,1,0:T(8,128)(2,1)S(1)} async-done(((bf16[4,256,256]{2,1,0:T(8,128)(2,1)}), bf16[4,256,256]{2,1,0:T(8,128)(2,1)S(1)}, u32[]{:S(2)}, u32[]{:S(2)}) %all-to-all-start.2) | async-done | bytes 524320 | tf_op jit(solution)/shard_map/all_to_all | solution.py:45
  35.3 0.0 copy-start.1
  35.3 5.1 %all-to-all-start = ((bf16[4,256,2048]{2,1,0:T(8,128)(2,1)}), bf16[4,256,2048]{2,1,0:T(8,128)(2,1)}, u32[]{:S(2)}, u32[]{:S(2)}) async-start(bf16[4,256,2048]{2,1,0:T(8,128)(2,1)} %bitcast.71), calls=%async_computation.1 | async-start | bytes 8388608 | tf_op jit(solution)/shard_map/all_to_all | solution.py:44
  40.3 0.0 copy-done.1
  40.4 0.3 convolution_bitcast_fusion.1
  40.6 92.4 %all-to-all-done = bf16[4,256,2048]{2,1,0:T(8,128)(2,1)} async-done(((bf16[4,256,2048]{2,1,0:T(8,128)(2,1)}), bf16[4,256,2048]{2,1,0:T(8,128)(2,1)}, u32[]{:S(2)}, u32[]{:S(2)}) %all-to-all-start) | async-done | bytes 4194336 | tf_op jit(solution)/shard_map/all_to_all | solution.py:44
  133.0 0.0 copy-done
  133.0 4.2 %fusion.9 = f32[4,8,32,64]{3,2,0,1:T(8,128)} fusion(bf16[8,2048,64]{1,2,0:T(8,128)(2,1)S(1)} %copy-done, bf16[4,8,32,2048]{3,2,1,0:T(8,128)(2,1)} %bitcast.7), kind=kOutput, calls=%fused_computation.17 | convolution fusion | flops 268435456 | bytes 6553600 | tf_op jit(solution)/shard_map/slcd,ldr->slcr/dot_general | solution.py:49
  137.3 26.1 %all-reduce.2 = (bf16[4,8,32,64]{3,2,0,1:T(8,128)(2,1)}, bf16[4,8,32,64]{3,2,0,1:T(8,128)(2,1)S(1)}) all-reduce(f32[4,8,32,64]{3,2,0,1:T(8,128)} %fusion.9, f32[4,8,32,64]{3,2,0,1:T(8,128)S(1)} %convolution_bitcast_fusion.1), channel_id=1, replica_groups=mesh['groups'=2,'dp'=4,'mp'=2,'sub'=2] {'mp','sub'}, use_global_device_ids=true, to_apply=%region_5.6 | all-reduce | flops 131072 | bytes 786432 | tf_op jit(solution)/shard_map/psum | solution.py:55
  163.4 1.3 fusion.8
  164.7 0.8 copy.14
  165.5 3.5 %all-to-all-start.1 = ((bf16[4,256,256]{2,1,0:T(8,128)(2,1)}), bf16[4,256,256]{2,1,0:T(8,128)(2,1)S(1)}, u32[]{:S(2)}, u32[]{:S(2)}) async-start(bf16[4,256,256]{2,1,0:T(8,128)(2,1)} %bitcast.75), calls=%async_computation.2 | async-start | bytes 1048576 | tf_op jit(solution)/shard_map/all_to_all | solution.py:77
  169.0 1.2 fusion.2
  170.2 2.3 copy.17
  172.5 11.7 %all-to-all-done.1 = bf16[4,256,256]{2,1,0:T(8,128)(2,1)S(1)} async-done(((bf16[4,256,256]{2,1,0:T(8,128)(2,1)}), bf16[4,256,256]{2,1,0:T(8,128)(2,1)S(1)}, u32[]{:S(2)}, u32[]{:S(2)}) %all-to-all-start.1) | async-done | bytes 524320 | tf_op jit(solution)/shard_map/all_to_all | solution.py:77
  184.2 4.9 %all-to-all-start.3 = ((bf16[4,256,2048]{2,1,0:T(8,128)(2,1)}), bf16[4,256,2048]{2,1,0:T(8,128)(2,1)}, u32[]{:S(2)}, u32[]{:S(2)}) async-start(bf16[4,256,2048]{2,1,0:T(8,128)(2,1)} %bitcast.70), calls=%async_computation.4 | async-start | bytes 8388608 | tf_op jit(solution)/shard_map/all_to_all | solution.py:84
  189.1 0.2 reduce-scatter.2.cloned.1.call-start
  189.3 6.6 %fusion.28 = f32[1024,512]{1,0:T(8,128)} fusion(bf16[2048,1024]{1,0:T(8,128)(2,1)} %param.7, bf16[512,2048]{1,0:T(8,128)(2,1)} %param.6), kind=kOutput, calls=%fused_computation.42 | convolution fusion | flops 2147483648 | bytes 8388608 | tf_op jit(solution)/shard_map/dot_general | solution.py:24
  195.9 0.0 reduce-scatter.2.cloned.1.call-update
  195.9 0.0 all-gather.2.cloned.1.call-start
  195.9 0.7 all-gather.2.cloned.1.call-update
  196.7 2.0 fusion.14
  198.7 5.0 %bitcast_multiply_fusion = f32[8,2048,64]{1,2,0:T(8,128)} fusion(bf16[4,8,32,2048]{3,2,1,0:T(8,128)(2,1)} %bitcast.7, bf16[4,8,32,64]{3,2,0,1:T(8,128)(2,1)S(1)} %get-tuple-element.13), kind=kOutput, calls=%fused_computation.5 | convolution fusion | flops 269484032 | bytes 8519680 | tf_op jit(solution)/shard_map/slcd,slcr->ldr/dot_general | solution.py:70
  203.7 1.9 gather_fusion
  205.6 0.1 copy.15
  205.8 22.9 %reduce-scatter.2.cloned.1.call-done = f32[256,512]{1,0:T(8,128)} async-done(((f32[1024,512]{1,0:T(8,128)}), f32[256,512]{1,0:T(8,128)}) %reduce-scatter.2.cloned.1.call-update) | async-done | bytes 524304 | tf_op jit(solution)/shard_map/reduce_scatter | solution.py:23
  228.7 1.1 fusion.15
  229.8 0.8 copy.20
  230.7 51.6 %all-to-all-done.3 = bf16[4,256,2048]{2,1,0:T(8,128)(2,1)} async-done(((bf16[4,256,2048]{2,1,0:T(8,128)(2,1)}), bf16[4,256,2048]{2,1,0:T(8,128)(2,1)}, u32[]{:S(2)}, u32[]{:S(2)}) %all-to-all-start.3) | async-done | bytes 4194336 | tf_op jit(solution)/shard_map/all_to_all | solution.py:84
  282.2 8.0 %gather_fusion.1 = bf16[512,2048]{1,0:T(8,128)(2,1)} fusion(bf16[1024,2048]{1,0:T(8,128)(2,1)} %bitcast.23, s32[1024]{0:T(1024)S(1)} %pad_clamp_fusion), kind=kCustom, calls=%fused_computation.1 | custom fusion | bytes 4196352 | tf_op jit(solution)/shard_map/gather | solution.py:95
  290.2 0.0 all-gather.2.cloned.1.call-done
  290.2 6.9 %add_convert_fusion = bf16[512,2048]{1,0:T(8,128)(2,1)} fusion(bf16[512,2048]{1,0:T(8,128)(2,1)} %gather_fusion.1, bf16[512,1024]{1,0:T(8,128)(2,1)} %all-gather.2.cloned.1.call-done, bf16[2048,1024]{1,0:T(8,128)(2,1)} %param.7), kind=kOutput, calls=%fused_computation.8 | convolution fusion | flops 2150629376 | bytes 9437184 | tf_op jit(solution)/shard_map/dot_general | solution.py:32
  (3 shorter events, 0.0 us)
Async XLA Ops:
  7.2 125.9 %copy-start = (bf16[8,2048,64]{1,2,0:T(8,128)(2,1)S(1)}, bf16[8,2048,64]{1,2,0:T(8,128)(2,1)}, u32[]{:S(2)}) copy-start(bf16[8,2048,64]{1,2,0:T(8,128)(2,1)} %param.8) | copy-start | bytes 6291460
  14.5 20.8 %all-to-all-start.2 = ((bf16[4,256,256]{2,1,0:T(8,128)(2,1)}), bf16[4,256,256]{2,1,0:T(8,128)(2,1)S(1)}, u32[]{:S(2)}, u32[]{:S(2)}) async-start(bf16[4,256,256]{2,1,0:T(8,128)(2,1)} %bitcast.16), calls=%async_computation.3 | async-start | bytes 1048576 | tf_op jit(solution)/shard_map/all_to_all | solution.py:45
  35.3 5.1 %copy-start.1 = (bf16[8,64,256]{2,1,0:T(8,128)(2,1)S(1)}, bf16[8,64,256]{2,1,0:T(8,128)(2,1)}, u32[]{:S(2)}) copy-start(bf16[8,64,256]{2,1,0:T(8,128)(2,1)} %param.9) | copy-start | bytes 786436
  35.3 97.8 %all-to-all-start = ((bf16[4,256,2048]{2,1,0:T(8,128)(2,1)}), bf16[4,256,2048]{2,1,0:T(8,128)(2,1)}, u32[]{:S(2)}, u32[]{:S(2)}) async-start(bf16[4,256,2048]{2,1,0:T(8,128)(2,1)} %bitcast.71), calls=%async_computation.1 | async-start | bytes 8388608 | tf_op jit(solution)/shard_map/all_to_all | solution.py:44
  165.5 18.7 %all-to-all-start.1 = ((bf16[4,256,256]{2,1,0:T(8,128)(2,1)}), bf16[4,256,256]{2,1,0:T(8,128)(2,1)S(1)}, u32[]{:S(2)}, u32[]{:S(2)}) async-start(bf16[4,256,256]{2,1,0:T(8,128)(2,1)} %bitcast.75), calls=%async_computation.2 | async-start | bytes 1048576 | tf_op jit(solution)/shard_map/all_to_all | solution.py:77
  184.2 98.0 %all-to-all-start.3 = ((bf16[4,256,2048]{2,1,0:T(8,128)(2,1)}), bf16[4,256,2048]{2,1,0:T(8,128)(2,1)}, u32[]{:S(2)}, u32[]{:S(2)}) async-start(bf16[4,256,2048]{2,1,0:T(8,128)(2,1)} %bitcast.70), calls=%async_computation.4 | async-start | bytes 8388608 | tf_op jit(solution)/shard_map/all_to_all | solution.py:84
  189.1 39.6 %reduce-scatter.2.cloned.1.call-start = ((), (), s32[]{:S(2)}) async-start(), calls=%async_computation.5 | async-start | bytes 2621440 | tf_op jit(solution)/shard_map/reduce_scatter | solution.py:23
  195.9 94.3 %all-gather.2.cloned.1.call-start = ((), (), s32[]{:S(2)}) async-start(), calls=%async_computation.6 | async-start | bytes 1310720 | tf_op jit(solution)/shard_map/all_gather | solution.py:33
Sparse Core Ops, SparseCore 0:
  196.0 32.6 reduce-scatter.1
  230.3 16.8 all-gather.1
where the time goes:
time: 305 us; the launch traced here: 304 us
  waiting for transfers between devices  186 us (61%)
  matrix products  27.5 us (9%)
  blocking collectives  26.1 us (9%)
  local copies, waits for them, and re-layouts  25.1 us (8%)
  starting transfers between devices  20 us (7%)
  between operations  14.1 us (5%)
  other arithmetic  4.63 us (2%)
    all_to_all x1, waiting for transfers between devices, local(): lax.all_to_all(send_x, 'dp', split_axis=0, concat_axis=0, tiled=True)  92.4 us
    all_to_all x1, waiting for transfers between devices, local(): lax.all_to_all(adapter_input_gradient.reshape(tenant_groups, resident_ten...  51.6 us
    psum x1, blocking collectives, local(): rank_output, rank_backward = lax.psum((partial_u, partial_v), ('mp', 'sub'))  26.1 us
    reduce_scatter x1, waiting for transfers between devices, local(): lax.psum_scatter(lax.dot_general(columns, tokens, (((0,), (1,)), ((), ())...  22.9 us
    all_to_all x1, waiting for transfers between devices, local(): lax.all_to_all(adapter_output.reshape(tenant_groups, resident_tenant * sl...  11.7 us
    gather x1, local copies, waits for them, and re-layouts, local(): back_dx.reshape(slots_count, slice_width_input)[target_output]  7.95 us
    scatter x1, local copies, waits for them, and re-layouts, local(): jnp.zeros((slots_count, slice_width_input), jnp.bfloat16).at[target_output]  7.29 us
    all_to_all x1, waiting for transfers between devices, local(): lax.all_to_all(send_g, 'dp', split_axis=0, concat_axis=0, tiled=True)  7.2 us
  transfers between devices with their start and end apart: 6, of which 5 were waited for; matrix products, arithmetic and copies ran while one was open for 12% of the time, Pallas kernels for 0%

commit v1 on v0

v1 whole, which is shorter than its diff:
```python
import jax
import jax.numpy as jnp
from jax import lax
from jax.sharding import PartitionSpec as P

adapter_scale = 0.5
f32 = jnp.float32
bf16 = jnp.bfloat16


def dot(a, b, ca, cb):
    return lax.dot_general(a, b, (((ca,), (cb,)), ((), ())), preferred_element_type=f32)


def local(tokens, base_weight, down, up, cotangent, tenant):
    groups = lax.axis_size("dp")
    own, width, rank = down.shape
    rows = tokens.shape[0]
    key_width = cotangent.shape[1]
    total = groups * own
    slots = own * (2 * rows // total)
    ids = tenant[:, 0]
    me = lax.axis_index("dp")
    down_rows = jnp.transpose(down, (0, 2, 1)).reshape(own * rank, width)
    up_rows = up.reshape(own * rank, key_width)

    holder = ids // own
    holds = (holder[:, None] == jnp.arange(groups, dtype=jnp.int32)[None, :]).astype(jnp.int32)
    place = jnp.sum(holds * (jnp.cumsum(holds, axis=0) - 1), axis=1)

    def shifted(array, step):
        if step == 0:
            return array
        return lax.ppermute(array, "dp", [(i, (i + step) % groups) for i in range(groups)])

    slot = jnp.arange(slots, dtype=jnp.int32)
    picks, x_in, g_in, own_in = [], [], [], []
    for step in range(groups):
        to = lax.rem(me + step, groups)
        pick = (holder[None, :] == to) & (place[None, :] == slot[:, None])
        tenant_of = jnp.max(jnp.where(pick, ids[None, :] - to * own, -1), axis=1)
        pick = pick.astype(bf16)
        picks.append(pick)
        own_in.append(shifted(tenant_of, step))
        g_in.append(shifted(dot(pick, cotangent, 1, 0).astype(bf16), step))
        x_in.append(shifted(dot(pick, tokens, 1, 0).astype(bf16), step))

    owner = jnp.arange(own * rank, dtype=jnp.int32) // rank
    masks = [t[:, None] == owner[None, :] for t in own_in]
    mask = jnp.concatenate(masks, 0)

    def fold(wide):
        return jnp.where(mask, wide, 0.0).reshape(-1, own, rank).sum(1)

    def spread(narrow):
        return jnp.where(mask, jnp.tile(narrow, (1, own)), jnp.zeros((), bf16))

    g_here = jnp.concatenate(g_in, 0)
    back = lax.psum(fold(dot(g_here, up_rows, 1, 1)), ("mp", "sub")).astype(bf16)
    back = spread(back)
    lora_dx = jnp.zeros((rows, width), f32)
    for step in range(groups):
        part = back[step * slots : (step + 1) * slots]
        term = (adapter_scale * dot(part, down_rows, 1, 0)).astype(bf16)
        term = shifted(term, (groups - step) % groups)
        lora_dx = lora_dx + dot(picks[step], term, 0, 0)

    x_here = jnp.concatenate(x_in, 0)
    out_rank = lax.psum(fold(dot(x_here, down_rows, 1, 1)), ("mp", "sub")).astype(bf16)
    out_rank = spread(out_rank)
    lora_out = jnp.zeros((rows, key_width), f32)
    for step in range(groups):
        part = out_rank[step * slots : (step + 1) * slots]
        term = (adapter_scale * dot(part, up_rows, 1, 0)).astype(bf16)
        term = shifted(term, (groups - step) % groups)
        lora_out = lora_out + dot(picks[step], term, 0, 0)

    down_grad = adapter_scale * dot(back, x_here, 0, 0)
    down_grad = jnp.transpose(down_grad.reshape(own, rank, width), (0, 2, 1))
    up_grad = (adapter_scale * dot(out_rank, g_here, 0, 0)).reshape(own, rank, key_width)

    frozen = lax.psum_scatter(
        dot(tokens, base_weight, 1, 0), ("mp", "sub"), scatter_dimension=1, tiled=True
    )
    g_wide = lax.all_gather(cotangent, ("mp", "sub"), axis=1, tiled=True)
    out = (frozen + lora_out).astype(bf16)
    token_grad = (dot(g_wide, base_weight, 1, 1) + lora_dx).astype(bf16)
    return out, token_grad, down_grad, up_grad


def solution(mesh):
    rows = P(("groups", "dp"), ("mp", "sub"))
    downs = P(("groups", "dp"), ("mp", "sub"), None)
    ups = P(("groups", "dp"), None, ("mp", "sub"))
    return jax.shard_map(
        local,
        mesh=mesh,
        in_specs=(rows, P(("mp", "sub"), None), downs, ups, rows, P(("groups", "dp"), None)),
        out_specs=(rows, rows, downs, ups),
        check_vma=False,
    )
```

time: 305 us -> 286 us (0.938)
  waiting for transfers between devices: 186 us -> 141 us
  matrix products: 27.5 us -> 58.5 us
  local copies, waits for them, and re-layouts: 25.1 us -> 1.58 us
  starting transfers between devices: 20 us -> 41.3 us
  blocking collectives: 26.1 us -> 17.8 us
  other arithmetic: 4.63 us -> 10.9 us
    all_to_all x4 -> x0, waiting for transfers between devices: 163 us -> none  [the longest x1 92.4 us: local(): lax.all_to_all(send_x, 'dp', split_axis=0, concat_axis=0, tiled=True)]
    ppermute x0 -> x15, waiting for transfers between devices: none -> 140 us  [shifted(): lax.ppermute(array, 'dp', [(i, (i + step) % groups) for i in range(groups)])]
    ppermute x0 -> x15, starting transfers between devices: none -> 41.2 us  [shifted(): lax.ppermute(array, 'dp', [(i, (i + step) % groups) for i in range(groups)])]
    dot_general x8 -> x28, matrix products: 27.5 us -> 58.5 us  [dot(): lax.dot_general(a, b, (((ca,), (cb,)), ((), ())), preferred_element_type=...]
    reduce_scatter x1, waiting for transfers between devices: 22.9 us -> 0.01 us  [local(): lax.psum_scatter(dot(tokens, base_weight, 1, 0), ('mp', 'sub'), scatter_d...]
    all_to_all x4 -> x0, starting transfers between devices: 19.7 us -> none  [the longest x1 6.32 us: local(): lax.all_to_all(send_g, 'dp', split_axis=0, concat_axis=0, tiled=True)]
    scatter x2 -> x0, local copies, waits for them, and re-layouts: 10.8 us -> none  [the longest x1 7.29 us: local(): jnp.zeros((slots_count, slice_width_input), jnp.bfloat16).at[target_output]]
    gather x3 -> x0, local copies, waits for them, and re-layouts: 10 us -> none  [the longest x1 7.95 us: local(): back_dx.reshape(slots_count, slice_width_input)[target_output]]
  transfers between devices with their start and end apart: 6 -> 17, of which waited for: 5 -> 3; matrix products, arithmetic and copies ran while one was open for 12% -> 24% of each run, Pallas kernels for 0% -> 0%
where the time goes in v1:
time: 286 us; the launch traced here: 285 us
  waiting for transfers between devices  141 us (49%)
  matrix products  58.5 us (20%)
  starting transfers between devices  41.3 us (14%)
  blocking collectives  17.8 us (6%)
  between operations  14.4 us (5%)
  other arithmetic  10.9 us (4%)
    ppermute x15, waiting for transfers between devices, shifted(): lax.ppermute(array, 'dp', [(i, (i + step) % groups) for i in range(groups)])  140 us
    dot_general x28, matrix products, dot(): lax.dot_general(a, b, (((ca,), (cb,)), ((), ())), preferred_element_type=...  58.5 us
    ppermute x15, starting transfers between devices, shifted(): lax.ppermute(array, 'dp', [(i, (i + step) % groups) for i in range(groups)])  41.2 us
    psum x1, blocking collectives, local(): lax.psum(fold(dot(x_here, down_rows, 1, 1)), ('mp', 'sub')).astype(bf16)  17.8 us
  transfers between devices with their start and end apart: 17, of which 3 were waited for; matrix products, arithmetic and copies ran while one was open for 24% of the time, Pallas kernels for 0%

profile of v1, /device:TPU:0, one launch (start us, length us, event | category | flops | bytes accessed | tf_op | source)
XLA Modules:
  0.0 285.1 jit_solution(726454341838898207)
XLA Ops:
  7.2 0.7 all-gather.2.cloned.1.call-update
  8.0 0.7 and_select_fusion
  8.7 0.7 broadcast_compare_fusion.7
  9.4 1.2 reduce-window.6
  11.1 0.8 broadcast_subtract_fusion.2
  11.9 1.0 select_reduce_fusion.3
  12.9 5.0 %collective-permute-start.2 = (s32[256]{0:T(256)S(1)}, s32[256]{0:T(256)S(1)}, u32[]{:S(2)}, u32[]{:S(2)}) collective-permute-start(s32[256]{0:T(256)S(1)} %get-tuple-element.5), channel_id=1, source_target_pairs={{0,12},{4,0},{8,4},{12,8},{1,13},{5,1},{9,5},{13,9},{2,14},{6,2},{... | collective-permute-start | bytes 3080 | tf_op jit(solution)/shard_map/ppermute | solution.py:34
  18.0 3.4 %convolution_convert_fusion = bf16[256,2048]{1,0:T(8,128)(2,1)} fusion(bf16[512,2048]{1,0:T(8,128)(2,1)} %param.6, s32[512]{0:T(512)S(1)} %fusion.84, pred[512]{0:T(512)(128)(4,1)S(1)} %get-tuple-element.24), kind=kOutput, calls=%fused_computation.11 | convolution fusion | flops 537657344 | bytes 3148288 | tf_op jit(solution)/shard_map/dot_general | solution.py:12
  21.3 0.4 collective-permute-start.5
  21.7 1.7 convolution_convert_fusion.1
  23.4 2.6 collective-permute-start.4
  26.0 1.7 convolution_convert_fusion.2
  27.7 2.0 collective-permute-start.3
  29.7 3.7 %fusion.97 = f32[512,1024]{1,0:T(8,128)} fusion(bf16[512,2048]{1,0:T(8,128)(2,1)S(1)} %copy-done.1, bf16[2048,1024]{1,0:T(8,128)(2,1)S(1)} %copy-done.13), kind=kOutput, calls=%fused_computation.140 | convolution fusion | flops 2147483648 | bytes 8388608 | tf_op jit(solution)/shard_map/dot_general | solution.py:12
  33.5 0.9 copy-done.8
  34.9 2.4 convolution_convert_fusion.3
  37.6 1.9 collective-permute-start.11
  40.0 56.0 %collective-permute-done = s32[256]{0:T(256)S(1)} collective-permute-done((s32[256]{0:T(256)S(1)}, s32[256]{0:T(256)S(1)}, u32[]{:S(2)}, u32[]{:S(2)}) %collective-permute-start) | collective-permute-done | bytes 1056 | tf_op jit(solution)/shard_map/ppermute | solution.py:34
  96.0 21.8 %collective-permute-start.10 = (bf16[256,256]{1,0:T(8,128)(2,1)S(1)}, bf16[256,256]{1,0:T(8,128)(2,1)S(1)}, u32[]{:S(2)}, u32[]{:S(2)}) collective-permute-start(bf16[256,256]{1,0:T(8,128)(2,1)S(1)} %convolution_convert_fusion.5), channel_id=1, source_target_pairs={{0,8},{4,12},{8,0},{12,4},{1,9},{5,13},{9,1},{13,5},{2,10},{6,14},... | collective-permute-start | bytes 393224 | tf_op jit(solution)/shard_map/ppermute | solution.py:34
  117.9 1.1 broadcast_compare_fusion.3
  119.0 8.1 %collective-permute-done.10 = bf16[256,256]{1,0:T(8,128)(2,1)S(1)} collective-permute-done((bf16[256,256]{1,0:T(8,128)(2,1)S(1)}, bf16[256,256]{1,0:T(8,128)(2,1)S(1)}, u32[]{:S(2)}, u32[]{:S(2)}) %collective-permute-start.10) | collective-permute-done | bytes 131104 | tf_op jit(solution)/shard_map/ppermute | solution.py:34
  127.1 1.8 convolution_select_fusion
  129.0 1.8 reduce_sum.29
  130.8 5.7 %convolution_select_fusion.1 = f32[1024,512]{0,1:T(8,128)} fusion(bf16[512,2048]{1,0:T(8,128)(2,1)S(1)} %bitcast.62, bf16[256,2048]{1,0:T(8,128)(2,1)} %collective-permute-done.5, bf16[256,2048]{1,0:T(8,128)(2,1)} %collective-permute-done.4, bf16[256,2048]{1,0:T(8,128)(2,1)} %collective-permute-done.3, bf16[256,2048]{1,0:T(8,128)(2,1)S(1)} %convolution_convert_fusion.3, ...), kind=kOutput, calls=%fused_computation.17 | convolution fusion | flops 2166358016 | bytes 8912896 | tf_op jit(solution)/shard_map/dot_general | solution.py:12
  136.5 1.7 reduce_sum.28
  138.2 17.8 %all-reduce.2 = (bf16[1024,64]{0,1:T(8,128)(2,1)}, bf16[1024,64]{0,1:T(8,128)(2,1)}) all-reduce(f32[1024,64]{0,1:T(8,128)S(1)} %reduce_sum.28, f32[1024,64]{0,1:T(8,128)S(1)} %reduce_sum.29), channel_id=1, replica_groups=mesh['groups'=2,'dp'=4,'mp'=2,'sub'=2] {'mp','sub'}, use_global_device_ids=true, to_apply=%region_9.10 | all-reduce | flops 131072 | bytes 786432 | tf_op jit(solution)/shard_map/psum | solution.py:69
  156.0 1.6 bitcast_select_fusion
  157.7 1.0 fusion.11
  158.7 1.0 fusion.10
  159.6 0.9 fusion.9
  160.6 1.8 fusion.3
  162.3 1.7 fusion.2
  164.1 1.8 fusion.1
  165.8 2.0 collective-permute-start.8
  167.9 2.4 collective-permute-start.12
  170.2 0.6 collective-permute-start.13
  170.8 1.2 convolution_multiply_fusion.5
  172.1 3.9 %fusion.4 = f32[512,2048]{1,0:T(8,128)} fusion(bf16[512,2048]{1,0:T(8,128)(2,1)S(1)} %bitcast.63, bf16[1024,512]{0,1:T(8,128)(2,1)S(1)} %get-tuple-element.12, s32[512]{0:T(512)S(1)} %fusion.84, pred[512]{0:T(512)(128)(4,1)} %copy-done.9), kind=kOutput, calls=%fused_computation.18 | convolution fusion | flops 1075052544 | bytes 6556160 | tf_op jit(solution)/shard_map/dot_general | solution.py:12
  176.0 6.5 %convolution_multiply_fusion = f32[512,2048]{1,0:T(8,128)} fusion(bf16[1024,512]{0,1:T(8,128)(2,1)S(1)} %get-tuple-element.12, bf16[256,2048]{1,0:T(8,128)(2,1)} %collective-permute-done.5, bf16[256,2048]{1,0:T(8,128)(2,1)} %collective-permute-done.4, bf16[256,2048]{1,0:T(8,128)(2,1)} %collective-permute-done.3, bf16[256,2048]{1,0:T(8,128)(2,1)} %copy-done.3), kind=kOutput, calls=%fused_computation.2 | convolution fusion | flops 2165309440 | bytes 9437184 | tf_op jit(solution)/shard_map/dot_general | solution.py:12
  182.6 1.6 fusion.12
  184.2 2.3 collective-permute-start.14
  186.8 0.4 fusion.35
  187.2 4.9 %fusion.98 = f32[512,2048]{1,0:T(8,128)S(1)} fusion(bf16[512,1024]{1,0:T(8,128)(2,1)} %all-gather.2.cloned.1.call-done, bf16[2048,1024]{1,0:T(8,128)(2,1)} %param.7), kind=kOutput, calls=%fused_computation.141 | convolution fusion | flops 2147483648 | bytes 9437184 | tf_op jit(solution)/shard_map/dot_general | solution.py:12
  192.1 75.6 %collective-permute-done.13 = bf16[256,2048]{1,0:T(8,128)(2,1)} collective-permute-done((bf16[256,2048]{1,0:T(8,128)(2,1)}, bf16[256,2048]{1,0:T(8,128)(2,1)}, u32[]{:S(2)}, u32[]{:S(2)}) %collective-permute-start.13) | collective-permute-done | bytes 1048608 | tf_op jit(solution)/shard_map/ppermute | solution.py:34
  267.7 2.0 fusion.27
  269.7 2.1 fusion.22
  272.2 3.9 %add_convert_fusion = bf16[512,2048]{1,0:T(8,128)(2,1)} fusion(f32[512,2048]{1,0:T(8,128)S(1)} %fusion.98, f32[512,2048]{1,0:T(8,128)S(1)} %fusion.27, f32[512,2048]{1,0:T(8,128)S(1)} %copy-done.2, f32[512,2048]{1,0:T(8,128)S(1)} %fusion.22, bf16[256,2048]{1,0:T(8,128)(2,1)} %collective-permute-done.14, s32[512]{0:T(512)S(1)} %fusion.84, ...), kind=kOutput, calls=%fused_computation.1 | convolution fusion | flops 542375936 | bytes 19925504 | tf_op jit(solution)/shard_map/dot_general | solution.py:12
  276.2 2.1 fusion.7
  (81 shorter events, 2.8 us)
Async XLA Ops:
  7.2 123.6 %copy-start = (bf16[8,2048,64]{1,2,0:T(8,128)(2,1)S(1)}, bf16[8,2048,64]{1,2,0:T(8,128)(2,1)}, u32[]{:S(2)}) copy-start(bf16[8,2048,64]{1,2,0:T(8,128)(2,1)} %param.8) | copy-start | bytes 6291460
  7.2 180.0 %all-gather.2.cloned.1.call-start = ((), (), s32[]{:S(2)}) async-start(), calls=%async_computation.2 | async-start | bytes 1310720 | tf_op jit(solution)/shard_map/all_gather | solution.py:85
  7.9 268.2 %reduce-scatter.2.cloned.1.call-start = ((), (), s32[]{:S(2)}) async-start(), calls=%async_computation.1 | async-start | bytes 2621440 | tf_op jit(solution)/shard_map/reduce_scatter | solution.py:82
  9.4 25.5 %copy-start.9 = (pred[512]{0:T(512)(128)(4,1)}, pred[512]{0:T(512)(128)(4,1)S(1)}, u32[]{:S(2)}) copy-start(pred[512]{0:T(512)(128)(4,1)S(1)} %get-tuple-element.10) | copy-start | bytes 1540
  11.0 10.7 %copy-start.1 = (bf16[512,2048]{1,0:T(8,128)(2,1)S(1)}, bf16[512,2048]{1,0:T(8,128)(2,1)}, u32[]{:S(2)}) copy-start(bf16[512,2048]{1,0:T(8,128)(2,1)} %param.6) | copy-start | bytes 6291460
  12.9 24.7 %collective-permute-start.2 = (s32[256]{0:T(256)S(1)}, s32[256]{0:T(256)S(1)}, u32[]{:S(2)}, u32[]{:S(2)}) collective-permute-start(s32[256]{0:T(256)S(1)} %get-tuple-element.5), channel_id=1, source_target_pairs={{0,12},{4,0},{8,4},{12,8},{1,13},{5,1},{9,5},{13,9},{2,14},{6,2},{... | collective-permute-start | bytes 3080 | tf_op jit(solution)/shard_map/ppermute | solution.py:34
  18.0 21.7 %collective-permute-start.1 = (s32[256]{0:T(256)S(1)}, s32[256]{0:T(256)S(1)}, u32[]{:S(2)}, u32[]{:S(2)}) collective-permute-start(s32[256]{0:T(256)S(1)} %get-tuple-element.6), channel_id=1, source_target_pairs={{0,8},{4,12},{8,0},{12,4},{1,9},{5,13},{9,1},{13,5},{2,10},{6,14},... | collective-permute-start | bytes 3080 | tf_op jit(solution)/shard_map/ppermute | solution.py:34
  21.3 109.4 %collective-permute-start.5 = (bf16[256,2048]{1,0:T(8,128)(2,1)}, bf16[256,2048]{1,0:T(8,128)(2,1)}, u32[]{:S(2)}, u32[]{:S(2)}) collective-permute-start(bf16[256,2048]{1,0:T(8,128)(2,1)} %convolution_convert_fusion), channel_id=1, source_target_pairs={{0,12},{4,0},{8,4},{12,8},{1,13},{5,1},{9,5},{13,9},{2,14},{6,2},{... | collective-permute-start | bytes 3145736 | tf_op jit(solution)/shard_map/ppermute | solution.py:34
  21.7 8.0 %copy-start.13 = (bf16[2048,1024]{1,0:T(8,128)(2,1)S(1)}, bf16[2048,1024]{1,0:T(8,128)(2,1)}, u32[]{:S(2)}) copy-start(bf16[2048,1024]{1,0:T(8,128)(2,1)} %param.7) | copy-start | bytes 12582916
  23.4 107.3 %collective-permute-start.4 = (bf16[256,2048]{1,0:T(8,128)(2,1)}, bf16[256,2048]{1,0:T(8,128)(2,1)}, u32[]{:S(2)}, u32[]{:S(2)}) collective-permute-start(bf16[256,2048]{1,0:T(8,128)(2,1)} %convolution_convert_fusion.1), channel_id=1, source_target_pairs={{0,8},{4,12},{8,0},{12,4},{1,9},{5,13},{9,1},{13,5},{2,10},{6,14},... | collective-permute-start | bytes 3145736 | tf_op jit(solution)/shard_map/ppermute | solution.py:34
  27.7 103.0 %collective-permute-start.3 = (bf16[256,2048]{1,0:T(8,128)(2,1)}, bf16[256,2048]{1,0:T(8,128)(2,1)}, u32[]{:S(2)}, u32[]{:S(2)}) collective-permute-start(bf16[256,2048]{1,0:T(8,128)(2,1)} %convolution_convert_fusion.2), channel_id=1, source_target_pairs={{0,4},{4,8},{8,12},{12,0},{1,5},{5,9},{9,13},{13,1},{2,6},{6,10},{... | collective-permute-start | bytes 3145736 | tf_op jit(solution)/shard_map/ppermute | solution.py:34
  33.5 0.9 copy-start.8
  34.7 92.5 %copy-start.22 = (bf16[256,256]{1,0:T(8,128)(2,1)}, bf16[256,256]{1,0:T(8,128)(2,1)S(1)}, u32[]{:S(2)}) copy-start(bf16[256,256]{1,0:T(8,128)(2,1)S(1)} %convolution_convert_fusion.7) | copy-start | bytes 393220
  34.9 82.9 %copy-start.10 = (s32[256]{0:T(256)S(1)}, s32[256]{0:T(256)}, u32[]{:S(2)}) copy-start(s32[256]{0:T(256)} %get-tuple-element.4) | copy-start | bytes 3076
  34.9 92.2 %copy-start.14 = (bf16[8,64,256]{2,1,0:T(8,128)(2,1)S(1)}, bf16[8,64,256]{2,1,0:T(8,128)(2,1)}, u32[]{:S(2)}) copy-start(bf16[8,64,256]{2,1,0:T(8,128)(2,1)} %param.9) | copy-start | bytes 786436
  37.3 93.4 %copy-start.3 = (bf16[256,2048]{1,0:T(8,128)(2,1)}, bf16[256,2048]{1,0:T(8,128)(2,1)S(1)}, u32[]{:S(2)}) copy-start(bf16[256,2048]{1,0:T(8,128)(2,1)S(1)} %convolution_convert_fusion.3) | copy-start | bytes 3145732
  37.6 80.3 %copy-start.11 = (s32[256]{0:T(256)}, s32[256]{0:T(256)S(1)}, u32[]{:S(2)}) copy-start(s32[256]{0:T(256)S(1)} %collective-permute-done.2) | copy-start | bytes 3076
  37.6 80.2 %collective-permute-start.11 = (bf16[256,256]{1,0:T(8,128)(2,1)S(1)}, bf16[256,256]{1,0:T(8,128)(2,1)S(1)}, u32[]{:S(2)}, u32[]{:S(2)}) collective-permute-start(bf16[256,256]{1,0:T(8,128)(2,1)S(1)} %convolution_convert_fusion.4), channel_id=1, source_target_pairs={{0,12},{4,0},{8,4},{12,8},{1,13},{5,1},{9,5},{13,9},{2,14},{6,2},{... | collective-permute-start | bytes 393224 | tf_op jit(solution)/shard_map/ppermute | solution.py:34
  39.7 78.2 %copy-start.12 = (s32[256]{0:T(256)}, s32[256]{0:T(256)S(1)}, u32[]{:S(2)}) copy-start(s32[256]{0:T(256)S(1)} %collective-permute-done.1) | copy-start | bytes 3076
  39.7 56.3 %collective-permute-start = (s32[256]{0:T(256)S(1)}, s32[256]{0:T(256)S(1)}, u32[]{:S(2)}, u32[]{:S(2)}) collective-permute-start(s32[256]{0:T(256)S(1)} %get-tuple-element.7), channel_id=1, source_target_pairs={{0,4},{4,8},{8,12},{12,0},{1,5},{5,9},{9,13},{13,1},{2,6},{6,10},{... | collective-permute-start | bytes 3080 | tf_op jit(solution)/shard_map/ppermute | solution.py:34
  96.0 31.1 %collective-permute-start.10 = (bf16[256,256]{1,0:T(8,128)(2,1)S(1)}, bf16[256,256]{1,0:T(8,128)(2,1)S(1)}, u32[]{:S(2)}, u32[]{:S(2)}) collective-permute-start(bf16[256,256]{1,0:T(8,128)(2,1)S(1)} %convolution_convert_fusion.5), channel_id=1, source_target_pairs={{0,8},{4,12},{8,0},{12,4},{1,9},{5,13},{9,1},{13,5},{2,10},{6,14},... | collective-permute-start | bytes 393224 | tf_op jit(solution)/shard_map/ppermute | solution.py:34
  117.8 11.1 %copy-start.16 = (bf16[256,256]{1,0:T(8,128)(2,1)}, bf16[256,256]{1,0:T(8,128)(2,1)S(1)}, u32[]{:S(2)}) copy-start(bf16[256,256]{1,0:T(8,128)(2,1)S(1)} %collective-permute-done.11) | copy-start | bytes 393220
  117.8 9.3 %collective-permute-start.9 = (bf16[256,256]{1,0:T(8,128)(2,1)S(1)}, bf16[256,256]{1,0:T(8,128)(2,1)S(1)}, u32[]{:S(2)}, u32[]{:S(2)}) collective-permute-start(bf16[256,256]{1,0:T(8,128)(2,1)S(1)} %convolution_convert_fusion.6), channel_id=1, source_target_pairs={{0,4},{4,8},{8,12},{12,0},{1,5},{5,9},{9,13},{13,1},{2,6},{6,10},{... | collective-permute-start | bytes 393224 | tf_op jit(solution)/shard_map/ppermute | solution.py:34
  118.9 10.0 %copy-start.5 = (pred[256,512]{0,1:T(32,128)(4,1)}, pred[256,512]{0,1:T(32,128)(4,1)S(1)}, u32[]{:S(2)}) copy-start(pred[256,512]{0,1:T(32,128)(4,1)S(1)} %get-tuple-element.15) | copy-start | bytes 393220
  118.9 10.0 %copy-start.6 = (pred[256,512]{0,1:T(32,128)(4,1)}, pred[256,512]{0,1:T(32,128)(4,1)S(1)}, u32[]{:S(2)}) copy-start(pred[256,512]{0,1:T(32,128)(4,1)S(1)} %get-tuple-element.16) | copy-start | bytes 393220
  119.0 10.0 %copy-start.7 = (pred[256,512]{0,1:T(32,128)(4,1)}, pred[256,512]{0,1:T(32,128)(4,1)S(1)}, u32[]{:S(2)}) copy-start(pred[256,512]{0,1:T(32,128)(4,1)S(1)} %get-tuple-element.17) | copy-start | bytes 393220
  127.1 1.8 copy-start.18
  127.1 1.8 copy-start.20
  156.0 1.7 copy-start.15
  157.7 13.1 %copy-start.4 = (bf16[1024,512]{0,1:T(8,128)(2,1)}, bf16[1024,512]{0,1:T(8,128)(2,1)S(1)}, u32[]{:S(2)}) copy-start(bf16[1024,512]{0,1:T(8,128)(2,1)S(1)} %get-tuple-element.13) | copy-start | bytes 3145732
  164.0 6.8 %copy-start.17 = (bf16[256,256]{1,0:T(8,128)(2,1)S(1)}, bf16[256,256]{1,0:T(8,128)(2,1)}, u32[]{:S(2)}) copy-start(bf16[256,256]{1,0:T(8,128)(2,1)} %copy-done.16) | copy-start | bytes 393220
  164.0 6.8 %copy-start.19 = (bf16[256,256]{1,0:T(8,128)(2,1)S(1)}, bf16[256,256]{1,0:T(8,128)(2,1)}, u32[]{:S(2)}) copy-start(bf16[256,256]{1,0:T(8,128)(2,1)} %copy-done.18) | copy-start | bytes 393220
  164.1 6.8 %copy-start.21 = (bf16[256,256]{1,0:T(8,128)(2,1)S(1)}, bf16[256,256]{1,0:T(8,128)(2,1)}, u32[]{:S(2)}) copy-start(bf16[256,256]{1,0:T(8,128)(2,1)} %copy-done.20) | copy-start | bytes 393220
  164.1 6.8 %copy-start.23 = (bf16[256,256]{1,0:T(8,128)(2,1)S(1)}, bf16[256,256]{1,0:T(8,128)(2,1)}, u32[]{:S(2)}) copy-start(bf16[256,256]{1,0:T(8,128)(2,1)} %copy-done.22) | copy-start | bytes 393220
  165.8 18.3 %collective-permute-start.6 = (bf16[256,256]{1,0:T(8,128)(2,1)}, bf16[256,256]{1,0:T(8,128)(2,1)S(1)}, u32[]{:S(2)}, u32[]{:S(2)}) collective-permute-start(bf16[256,256]{1,0:T(8,128)(2,1)} %fusion.9), channel_id=1, source_target_pairs={{0,12},{4,0},{8,4},{12,8},{1,13},{5,1},{9,5},{13,9},{2,14},{6,2},{... | collective-permute-start | bytes 393224 | tf_op jit(solution)/shard_map/ppermute | solution.py:34
  165.8 110.3 %collective-permute-start.7 = (bf16[256,256]{1,0:T(8,128)(2,1)}, bf16[256,256]{1,0:T(8,128)(2,1)S(1)}, u32[]{:S(2)}, u32[]{:S(2)}) collective-permute-start(bf16[256,256]{1,0:T(8,128)(2,1)} %fusion.10), channel_id=1, source_target_pairs={{0,8},{4,12},{8,0},{12,4},{1,9},{5,13},{9,1},{13,5},{2,10},{6,14},... | collective-permute-start | bytes 393224 | tf_op jit(solution)/shard_map/ppermute | solution.py:34
  165.8 21.0 %collective-permute-start.8 = (bf16[256,256]{1,0:T(8,128)(2,1)}, bf16[256,256]{1,0:T(8,128)(2,1)S(1)}, u32[]{:S(2)}, u32[]{:S(2)}) collective-permute-start(bf16[256,256]{1,0:T(8,128)(2,1)} %fusion.11), channel_id=1, source_target_pairs={{0,4},{4,8},{8,12},{12,0},{1,5},{5,9},{9,13},{13,1},{2,6},{6,10},{... | collective-permute-start | bytes 393224 | tf_op jit(solution)/shard_map/ppermute | solution.py:34
  167.9 101.8 %collective-permute-start.12 = (bf16[256,2048]{1,0:T(8,128)(2,1)}, bf16[256,2048]{1,0:T(8,128)(2,1)}, u32[]{:S(2)}, u32[]{:S(2)}) collective-permute-start(bf16[256,2048]{1,0:T(8,128)(2,1)} %fusion.1), channel_id=1, source_target_pairs={{0,12},{4,0},{8,4},{12,8},{1,13},{5,1},{9,5},{13,9},{2,14},{6,2},{... | collective-permute-start | bytes 3145736 | tf_op jit(solution)/shard_map/ppermute | solution.py:34
  170.2 97.5 %collective-permute-start.13 = (bf16[256,2048]{1,0:T(8,128)(2,1)}, bf16[256,2048]{1,0:T(8,128)(2,1)}, u32[]{:S(2)}, u32[]{:S(2)}) collective-permute-start(bf16[256,2048]{1,0:T(8,128)(2,1)} %fusion.2), channel_id=1, source_target_pairs={{0,8},{4,12},{8,0},{12,4},{1,9},{5,13},{9,1},{13,5},{2,10},{6,14},... | collective-permute-start | bytes 3145736 | tf_op jit(solution)/shard_map/ppermute | solution.py:34
  184.2 87.7 %collective-permute-start.14 = (bf16[256,2048]{1,0:T(8,128)(2,1)}, bf16[256,2048]{1,0:T(8,128)(2,1)}, u32[]{:S(2)}, u32[]{:S(2)}) collective-permute-start(bf16[256,2048]{1,0:T(8,128)(2,1)} %fusion.3), channel_id=1, source_target_pairs={{0,4},{4,8},{8,12},{12,0},{1,5},{5,9},{9,13},{13,1},{2,6},{6,10},{... | collective-permute-start | bytes 3145736 | tf_op jit(solution)/shard_map/ppermute | solution.py:34
  269.7 2.5 copy-start.2
Sparse Core Ops, SparseCore 0:
  9.6 19.5 all-gather.1
  33.6 30.8 reduce-scatter.1

commit v2 on v1

v2 whole, which is shorter than its diff:
```python
import jax
import jax.numpy as jnp
from jax import lax
from jax.sharding import PartitionSpec as P

adapter_scale = 0.5
f32 = jnp.float32
bf16 = jnp.bfloat16


def dot(a, b, ca, cb):
    return lax.dot_general(a, b, (((ca,), (cb,)), ((), ())), preferred_element_type=f32)


def body(tokens, base_weight, down, up, cotangent, ids, holder, place, slots):
    groups = lax.axis_size("dp")
    own, width, rank = down.shape
    rows = tokens.shape[0]
    key_width = cotangent.shape[1]
    me = lax.axis_index("dp")
    down_rows = jnp.transpose(down, (0, 2, 1)).reshape(own * rank, width)
    up_rows = up.reshape(own * rank, key_width)

    def shifted(array, step):
        if step == 0:
            return array
        return lax.ppermute(array, "dp", [(i, (i + step) % groups) for i in range(groups)])

    slot = jnp.arange(slots, dtype=jnp.int32)
    steps = [(2 * groups - 1 - k) % groups for k in range(groups)]
    picks, x_in, g_in, own_in = {}, {}, {}, {}
    for step in steps:
        to = lax.rem(me + step, groups)
        pick = (holder[None, :] == to) & (place[None, :] == slot[:, None])
        tenant_of = jnp.max(jnp.where(pick, ids[None, :] - to * own, -1), axis=1)
        picks[step] = pick.astype(bf16)
        own_in[step] = shifted(tenant_of, step)
        g_in[step] = dot(picks[step], cotangent, 1, 0).astype(bf16)
    packed, tokens_later = lax.optimization_barrier((g_in, tokens))
    for step in steps:
        g_in[step] = shifted(packed[step], step)
        x_in[step] = shifted(dot(picks[step], tokens_later, 1, 0).astype(bf16), step)

    owner = jnp.arange(own * rank, dtype=jnp.int32) // rank
    mask = jnp.concatenate([own_in[s] for s in steps], 0)[:, None] == owner[None, :]

    def fold(wide):
        return jnp.where(mask, wide, 0.0).reshape(-1, own, rank).sum(1)

    def spread(narrow):
        return jnp.where(mask, jnp.tile(narrow, (1, own)), jnp.zeros((), bf16))

    g_here = jnp.concatenate([g_in[s] for s in steps], 0)
    back = lax.psum(fold(dot(g_here, up_rows, 1, 1)), ("mp", "sub")).astype(bf16)
    back = spread(back)
    terms = []
    for k, step in enumerate(steps):
        part = back[k * slots : (k + 1) * slots]
        term = (adapter_scale * dot(part, down_rows, 1, 0)).astype(bf16)
        terms.append(term)
    terms = [shifted(t, (groups - s) % groups) for t, s in zip(terms, steps)]

    x_here = jnp.concatenate([x_in[s] for s in steps], 0)
    x_here, back = lax.optimization_barrier((x_here, back))
    out_rank = lax.psum(fold(dot(x_here, down_rows, 1, 1)), ("mp", "sub")).astype(bf16)
    out_rank = spread(out_rank)
    lora_out = jnp.zeros((rows, key_width), f32)
    for k, step in enumerate(steps):
        part = out_rank[k * slots : (k + 1) * slots]
        term = (adapter_scale * dot(part, up_rows, 1, 0)).astype(bf16)
        term = shifted(term, (groups - step) % groups)
        lora_out = lora_out + dot(picks[step], term, 0, 0)

    down_grad = adapter_scale * dot(back, x_here, 0, 0)
    down_grad = jnp.transpose(down_grad.reshape(own, rank, width), (0, 2, 1))
    up_grad = (adapter_scale * dot(out_rank, g_here, 0, 0)).reshape(own, rank, key_width)

    frozen = lax.psum_scatter(
        dot(tokens, base_weight, 1, 0), ("mp", "sub"), scatter_dimension=1, tiled=True
    )
    g_wide = lax.all_gather(cotangent, ("mp", "sub"), axis=1, tiled=True)
    out = (frozen + lora_out).astype(bf16)
    dx = dot(g_wide, base_weight, 1, 1)
    for step, term in zip(steps, terms):
        dx = dx + dot(picks[step], term, 0, 0)
    return out, dx.astype(bf16), down_grad, up_grad


def local(tokens, base_weight, down, up, cotangent, tenant):
    groups = lax.axis_size("dp")
    own = down.shape[0]
    most = own * (2 * tokens.shape[0] // (groups * own))
    usual = -(-(most * 3 // 4) // 16) * 16
    ids = tenant[:, 0]
    holder = ids // own
    holds = (holder[:, None] == jnp.arange(groups, dtype=jnp.int32)[None, :]).astype(jnp.int32)
    place = jnp.sum(holds * (jnp.cumsum(holds, axis=0) - 1), axis=1)
    args = (tokens, base_weight, down, up, cotangent, ids, holder, place)
    if usual >= most:
        return body(*args, most)
    results = body(*args, usual)
    fullest = lax.pmax(jnp.max(place), ("groups", "dp"))
    return lax.cond(fullest >= usual, lambda r: body(*args, most), lambda r: r, results)


def solution(mesh):
    rows = P(("groups", "dp"), ("mp", "sub"))
    downs = P(("groups", "dp"), ("mp", "sub"), None)
    ups = P(("groups", "dp"), None, ("mp", "sub"))
    return jax.shard_map(
        local,
        mesh=mesh,
        in_specs=(rows, P(("mp", "sub"), None), downs, ups, rows, P(("groups", "dp"), None)),
        out_specs=(rows, rows, downs, ups),
        check_vma=False,
    )
```

time: 286 us -> 231 us (0.81)
  waiting for transfers between devices: 141 us -> 44.9 us
  blocking collectives: 17.8 us -> 37.8 us
  starting transfers between devices: 41.3 us -> 50.3 us
  matrix products: 58.5 us -> 65 us
  other arithmetic: 10.9 us -> 14.8 us
    ppermute x15, waiting for transfers between devices: 140 us -> 44.1 us  [shifted(): lax.ppermute(array, 'dp', [(i, (i + step) % groups) for i in range(groups)])]
    pmax x0 -> x1, blocking collectives: none -> 10.6 us  [local(): fullest = lax.pmax(jnp.max(place), ('groups', 'dp'))]
    psum x1 -> x2, blocking collectives: 17.8 us -> 27.2 us  [the longest x1 14.2 us: body(): lax.psum(fold(dot(x_here, down_rows, 1, 1)), ('mp', 'sub')).astype(bf16)]
    ppermute x15, starting transfers between devices: 41.2 us -> 50.2 us  [shifted(): lax.ppermute(array, 'dp', [(i, (i + step) % groups) for i in range(groups)])]
    dot_general x28, matrix products: 58.5 us -> 65 us  [dot(): lax.dot_general(a, b, (((ca,), (cb,)), ((), ())), preferred_element_type=...]
  transfers between devices with their start and end apart: 17 -> 17, of which waited for: 3 -> 2; matrix products, arithmetic and copies ran while one was open for 24% -> 33% of each run, Pallas kernels for 0% -> 0%
where the time goes in v2:
time: 231 us; the launch traced here: 230 us
  matrix products  65 us (28%)
  starting transfers between devices  50.3 us (22%)
  waiting for transfers between devices  44.9 us (19%)
  blocking collectives  37.8 us (16%)
  between operations  15.1 us (7%)
  other arithmetic  14.8 us (6%)
    dot_general x28, matrix products, dot(): lax.dot_general(a, b, (((ca,), (cb,)), ((), ())), preferred_element_type=...  65 us
    ppermute x15, starting transfers between devices, shifted(): lax.ppermute(array, 'dp', [(i, (i + step) % groups) for i in range(groups)])  50.2 us
    ppermute x15, waiting for transfers between devices, shifted(): lax.ppermute(array, 'dp', [(i, (i + step) % groups) for i in range(groups)])  44.1 us
    psum x1, blocking collectives, body(): lax.psum(fold(dot(x_here, down_rows, 1, 1)), ('mp', 'sub')).astype(bf16)  14.2 us
    psum x1, blocking collectives, body(): lax.psum(fold(dot(g_here, up_rows, 1, 1)), ('mp', 'sub')).astype(bf16)  13 us
    pmax x1, blocking collectives, local(): fullest = lax.pmax(jnp.max(place), ('groups', 'dp'))  10.6 us
  transfers between devices with their start and end apart: 17, of which 2 were waited for; matrix products, arithmetic and copies ran while one was open for 33% of the time, Pallas kernels for 0%

profile of v2, /device:TPU:0, one launch (start us, length us, event | category | flops | bytes accessed | tf_op | source)
XLA Modules:
  0.0 230.1 jit_solution(10207869318638576463)
XLA Ops:
  10.0 1.2 reduce-window.6
  12.7 5.1 %collective-permute-start.15 = (s32[192]{0:T(256)S(1)}, s32[192]{0:T(256)S(1)}, u32[]{:S(2)}, u32[]{:S(2)}) collective-permute-start(s32[192]{0:T(256)S(1)} %get-tuple-element.85), channel_id=1, source_target_pairs={{0,12},{4,0},{8,4},{12,8},{1,13},{5,1},{9,5},{13,9},{2,14},{6,2},{... | collective-permute-start | bytes 2312 | tf_op jit(solution)/shard_map/ppermute | solution.py:27
  17.8 1.0 collective-permute-start.16
  18.9 1.2 convolution_convert_fusion.12
  20.0 1.2 convolution_convert_fusion.13
  21.2 1.2 convolution_convert_fusion.14
  22.4 1.2 convolution_convert_fusion.15
  23.6 2.9 %collective-permute-start.21 = (bf16[192,256]{1,0:T(8,128)(2,1)S(1)}, bf16[192,256]{1,0:T(8,128)(2,1)S(1)}, u32[]{:S(2)}, u32[]{:S(2)}) collective-permute-start(bf16[192,256]{1,0:T(8,128)(2,1)S(1)} %convolution_convert_fusion.12), channel_id=1, source_target_pairs={{0,12},{4,0},{8,4},{12,8},{1,13},{5,1},{9,5},{13,9},{2,14},{6,2},{... | collective-permute-start | bytes 294920 | tf_op jit(solution)/shard_map/ppermute | solution.py:27
  26.4 2.0 collective-permute-start.22
  28.5 5.9 %fusion.189 = f32[512,1024]{1,0:T(8,128)} fusion(bf16[512,2048]{1,0:T(8,128)(2,1)S(1)} %copy-done, bf16[2048,1024]{1,0:T(8,128)(2,1)} %param.9), kind=kOutput, calls=%fused_computation.256 | convolution fusion | flops 2147483648 | bytes 8388608 | tf_op jit(solution)/shard_map/dot_general | solution.py:12
  34.4 1.5 convolution_convert_fusion.8
  35.8 1.5 convolution_convert_fusion.9
  37.3 1.5 convolution_convert_fusion.10
  38.8 1.5 convolution_convert_fusion.11
  40.9 10.6 %pmax.7 = s32[]{:T(128)} all-reduce(s32[]{:T(128)} %reduce_max.81), channel_id=1, replica_groups=mesh['groups'=2,'dp'=4,'mp'=2,'sub'=2] {'groups','dp'}, use_global_device_ids=true, to_apply=%region_4.5 | all-reduce | flops 1 | bytes 8 | tf_op jit(solution)/shard_map/pmax | solution.py:102
  52.8 3.2 %collective-permute-start.18 = (bf16[192,2048]{1,0:T(8,128)(2,1)}, bf16[192,2048]{1,0:T(8,128)(2,1)}, u32[]{:S(2)}, u32[]{:S(2)}) collective-permute-start(bf16[192,2048]{1,0:T(8,128)(2,1)} %convolution_convert_fusion.11), channel_id=1, source_target_pairs={{0,12},{4,0},{8,4},{12,8},{1,13},{5,1},{9,5},{13,9},{2,14},{6,2},{... | collective-permute-start | bytes 2359304 | tf_op jit(solution)/shard_map/ppermute | solution.py:27
  56.8 3.0 %collective-permute-done.23 = bf16[192,256]{1,0:T(8,128)(2,1)S(1)} collective-permute-done((bf16[192,256]{1,0:T(8,128)(2,1)S(1)}, bf16[192,256]{1,0:T(8,128)(2,1)S(1)}, u32[]{:S(2)}, u32[]{:S(2)}) %collective-permute-start.23) | collective-permute-done | bytes 98336 | tf_op jit(solution)/shard_map/ppermute | solution.py:27
  59.8 1.6 compare_select_fusion.7
  61.3 1.5 reduce_sum.46
  62.9 13.0 %all-reduce.6 = bf16[768,64]{0,1:T(8,128)(2,1)} all-reduce(f32[768,64]{0,1:T(8,128)S(1)} %reduce_sum.46), channel_id=1, replica_groups=mesh['groups'=2,'dp'=4,'mp'=2,'sub'=2] {'mp','sub'}, use_global_device_ids=true, to_apply=%region_11.12 | all-reduce | flops 49152 | bytes 294912 | tf_op jit(solution)/shard_map/psum | solution.py:54
  75.9 1.3 compare_select_fusion.6
  77.2 3.2 %fusion.91 = bf16[192,2048]{1,0:T(8,128)(2,1)} fusion(bf16[512,2048]{1,0:T(8,128)(2,1)} %bitcast.117, bf16[768,512]{0,1:T(8,128)(2,1)S(1)} %compare_select_fusion.6), kind=kOutput, calls=%fused_computation.128 | convolution fusion | flops 403439616 | bytes 3145728 | tf_op jit(solution)/shard_map/dot_general | solution.py:12
  80.4 1.5 fusion.90
  81.9 26.5 %collective-permute-start.27 = (bf16[192,2048]{1,0:T(8,128)(2,1)}, bf16[192,2048]{1,0:T(8,128)(2,1)}, u32[]{:S(2)}, u32[]{:S(2)}) collective-permute-start(bf16[192,2048]{1,0:T(8,128)(2,1)} %fusion.90), channel_id=1, source_target_pairs={{0,4},{4,8},{8,12},{12,0},{1,5},{5,9},{9,13},{13,1},{2,6},{6,10},{... | collective-permute-start | bytes 2359304 | tf_op jit(solution)/shard_map/ppermute | solution.py:27
  108.4 1.4 collective-permute-start.28
  109.9 1.5 fusion.92
  111.4 4.8 %fusion.94 = f32[512,2048]{1,0:T(8,128)} fusion(bf16[512,2048]{1,0:T(8,128)(2,1)} %bitcast.118, bf16[768,512]{0,1:T(8,128)(2,1)S(1)} %compare_select_fusion.6, s32[512]{0:T(512)S(1)} %fusion.176, pred[512]{0:T(512)(128)(4,1)} %copy-done.36), kind=kOutput, calls=%fused_computation.135 | convolution fusion | flops 806289408 | bytes 6556160 | tf_op jit(solution)/shard_map/dot_general | solution.py:12
  116.1 2.9 %collective-permute-start.29 = (bf16[192,2048]{1,0:T(8,128)(2,1)}, bf16[192,2048]{1,0:T(8,128)(2,1)}, u32[]{:S(2)}, u32[]{:S(2)}) collective-permute-start(bf16[192,2048]{1,0:T(8,128)(2,1)} %fusion.92), channel_id=1, source_target_pairs={{0,12},{4,0},{8,4},{12,8},{1,13},{5,1},{9,5},{13,9},{2,14},{6,2},{... | collective-permute-start | bytes 2359304 | tf_op jit(solution)/shard_map/ppermute | solution.py:27
  119.1 41.1 %collective-permute-done.19 = bf16[192,2048]{1,0:T(8,128)(2,1)} collective-permute-done((bf16[192,2048]{1,0:T(8,128)(2,1)}, bf16[192,2048]{1,0:T(8,128)(2,1)}, u32[]{:S(2)}, u32[]{:S(2)}) %collective-permute-start.19) | collective-permute-done | bytes 786464 | tf_op jit(solution)/shard_map/ppermute | solution.py:27
  160.2 2.0 pad_maximum_fusion.1
  162.2 3.0 %compare_select_fusion.5 = f32[768,512]{0,1:T(8,128)} fusion(bf16[768,2048]{1,0:T(8,128)(2,1)S(1)} %pad_maximum_fusion.1, bf16[512,2048]{1,0:T(8,128)(2,1)S(1)} %bitcast.121, s32[768]{0:T(1024)S(1)} %pad_add_fusion.1, s32[512]{0:T(512)S(1)} %add_select_fusion.1), kind=kOutput, calls=%fused_computation.120 | convolution fusion | flops 1611399168 | bytes 6820864 | tf_op jit(solution)/shard_map/dot_general | solution.py:12
  165.2 2.2 reduce_sum.47
  167.4 14.2 %all-reduce.7 = bf16[768,64]{0,1:T(8,128)(2,1)} all-reduce(f32[768,64]{0,1:T(8,128)} %reduce_sum.47), channel_id=1, replica_groups=mesh['groups'=2,'dp'=4,'mp'=2,'sub'=2] {'mp','sub'}, use_global_device_ids=true, to_apply=%region_13.14 | all-reduce | flops 49152 | bytes 294912 | tf_op jit(solution)/shard_map/psum | solution.py:65
  181.6 1.1 compare_select_fusion.4
  182.7 0.9 fusion.101
  183.6 1.0 fusion.100
  184.6 2.4 %fusion.103 = f32[512,256]{1,0:T(8,128)} fusion(bf16[512,256]{1,0:T(8,128)(2,1)S(1)} %bitcast.134, bf16[768,512]{0,1:T(8,128)(2,1)} %copy-done.14, s32[512]{0:T(512)S(1)} %fusion.176, pred[512]{0:T(512)(128)(4,1)} %copy-done.36), kind=kOutput, calls=%fused_computation.153 | convolution fusion | flops 100958208 | bytes 1051136 | tf_op jit(solution)/shard_map/dot_general | solution.py:12
  187.0 1.8 fusion.99
  188.8 2.3 fusion.188
  191.1 5.7 %convolution_multiply_fusion.9 = f32[512,2048]{1,0:T(8,128)} fusion(bf16[768,512]{0,1:T(8,128)(2,1)S(1)} %compare_select_fusion.6, bf16[768,2048]{1,0:T(8,128)(2,1)} %copy-done.13), kind=kOutput, calls=%fused_computation.117 | convolution fusion | flops 1611661312 | bytes 8126464 | tf_op jit(solution)/shard_map/dot_general | solution.py:12
  196.9 3.9 %collective-permute-start.26 = (bf16[192,256]{1,0:T(8,128)(2,1)S(1)}, bf16[192,256]{1,0:T(8,128)(2,1)S(1)}, u32[]{:S(2)}, u32[]{:S(2)}) collective-permute-start(bf16[192,256]{1,0:T(8,128)(2,1)S(1)} %copy-done.39), channel_id=1, source_target_pairs={{0,12},{4,0},{8,4},{12,8},{1,13},{5,1},{9,5},{13,9},{2,14},{6,2},{... | collective-permute-start | bytes 294920 | tf_op jit(solution)/shard_map/ppermute | solution.py:27
  200.8 3.9 %fusion.109 = f32[512,2048]{1,0:T(8,128)} fusion(bf16[192,2048]{1,0:T(8,128)(2,1)} %collective-permute-done.27, s32[512]{0:T(512)S(1)} %fusion.176, pred[512]{0:T(512)(128)(4,1)S(1)} %get-tuple-element.105), kind=kOutput, calls=%fused_computation.164 | convolution fusion | flops 402849792 | bytes 4983296 | tf_op jit(solution)/shard_map/dot_general | solution.py:12
  204.7 3.9 %fusion.114 = f32[512,2048]{1,0:T(8,128)} fusion(bf16[192,2048]{1,0:T(8,128)(2,1)} %collective-permute-done.28, s32[512]{0:T(512)S(1)} %fusion.176, pred[512]{0:T(512)(128)(4,1)S(1)} %copy-done.35), kind=kOutput, calls=%fused_computation.165 | convolution fusion | flops 402849792 | bytes 4983296 | tf_op jit(solution)/shard_map/dot_general | solution.py:12
  209.3 5.0 %fusion.190 = f32[512,2048]{1,0:T(8,128)S(1)} fusion(bf16[512,1024]{1,0:T(8,128)(2,1)} %all-gather.5.cloned.1.call-done, bf16[2048,1024]{1,0:T(8,128)(2,1)} %param.9), kind=kOutput, calls=%fused_computation.257 | convolution fusion | flops 2147483648 | bytes 9437184 | tf_op jit(solution)/shard_map/dot_general | solution.py:12
  214.4 1.1 copy-done.9
  215.5 3.8 %add_convert_fusion.1 = bf16[512,2048]{1,0:T(8,128)(2,1)} fusion(f32[512,2048]{1,0:T(8,128)S(1)} %copy-done.7, f32[512,2048]{1,0:T(8,128)S(1)} %copy-done.9, f32[512,2048]{1,0:T(8,128)S(1)} %fusion.190, f32[512,2048]{1,0:T(8,128)S(1)} %copy-done.8, bf16[192,2048]{1,0:T(8,128)(2,1)} %collective-permute-done.29, s32[512]{0:T(512)S(1)} %fusion.176, ...), kind=kOutput, calls=%fused_computation.116 | convolution fusion | flops 408092672 | bytes 19663360 | tf_op jit(solution)/shard_map/dot_general | solution.py:12
  219.3 1.6 fusion.98
  221.3 2.0 broadcast_multiply_fusion
  (84 shorter events, 7.5 us)
Async XLA Ops:
  7.2 21.3 %copy-start = (bf16[512,2048]{1,0:T(8,128)(2,1)S(1)}, bf16[512,2048]{1,0:T(8,128)(2,1)}, u32[]{:S(2)}) copy-start(bf16[512,2048]{1,0:T(8,128)(2,1)} %param.8) | copy-start | bytes 6291460
  7.2 202.1 %all-gather.5.cloned.1.call-start = ((), (), s32[]{:S(2)}) async-start(), calls=%async_computation.5 | async-start | bytes 1310720 | tf_op jit(solution)/shard_map/all_gather | solution.py:81
  7.9 211.4 %reduce-scatter.5.cloned.1.call-start = ((), (), s32[]{:S(2)}) async-start(), calls=%async_computation.4 | async-start | bytes 2621440 | tf_op jit(solution)/shard_map/reduce_scatter | solution.py:78
  9.4 0.6 copy-start.25
  9.4 27.9 %copy-start.34 = (pred[512]{0:T(512)(128)(4,1)}, pred[512]{0:T(512)(128)(4,1)S(1)}, u32[]{:S(2)}) copy-start(pred[512]{0:T(512)(128)(4,1)S(1)} %get-tuple-element.89) | copy-start | bytes 1540
  9.4 25.0 %copy-start.36 = (pred[512]{0:T(512)(128)(4,1)}, pred[512]{0:T(512)(128)(4,1)S(1)}, u32[]{:S(2)}) copy-start(pred[512]{0:T(512)(128)(4,1)S(1)} %get-tuple-element.104) | copy-start | bytes 1540
  9.4 26.4 %copy-start.32 = (pred[512]{0:T(512)(128)(4,1)}, pred[512]{0:T(512)(128)(4,1)S(1)}, u32[]{:S(2)}) copy-start(pred[512]{0:T(512)(128)(4,1)S(1)} %get-tuple-element.103) | copy-start | bytes 1540
  12.7 39.4 %collective-permute-start.15 = (s32[192]{0:T(256)S(1)}, s32[192]{0:T(256)S(1)}, u32[]{:S(2)}, u32[]{:S(2)}) collective-permute-start(s32[192]{0:T(256)S(1)} %get-tuple-element.85), channel_id=1, source_target_pairs={{0,12},{4,0},{8,4},{12,8},{1,13},{5,1},{9,5},{13,9},{2,14},{6,2},{... | collective-permute-start | bytes 2312 | tf_op jit(solution)/shard_map/ppermute | solution.py:27
  17.8 35.0 %collective-permute-start.17 = (s32[192]{0:T(256)S(1)}, s32[192]{0:T(256)S(1)}, u32[]{:S(2)}, u32[]{:S(2)}) collective-permute-start(s32[192]{0:T(256)S(1)} %get-tuple-element.87), channel_id=1, source_target_pairs={{0,4},{4,8},{8,12},{12,0},{1,5},{5,9},{9,13},{13,1},{2,6},{6,10},{... | collective-permute-start | bytes 2312 | tf_op jit(solution)/shard_map/ppermute | solution.py:27
  17.8 38.2 %collective-permute-start.16 = (s32[192]{0:T(256)S(1)}, s32[192]{0:T(256)S(1)}, u32[]{:S(2)}, u32[]{:S(2)}) collective-permute-start(s32[192]{0:T(256)S(1)} %get-tuple-element.88), channel_id=1, source_target_pairs={{0,8},{4,12},{8,0},{12,4},{1,9},{5,13},{9,1},{13,5},{2,10},{6,14},... | collective-permute-start | bytes 2312 | tf_op jit(solution)/shard_map/ppermute | solution.py:27
  23.6 32.7 %collective-permute-start.21 = (bf16[192,256]{1,0:T(8,128)(2,1)S(1)}, bf16[192,256]{1,0:T(8,128)(2,1)S(1)}, u32[]{:S(2)}, u32[]{:S(2)}) collective-permute-start(bf16[192,256]{1,0:T(8,128)(2,1)S(1)} %convolution_convert_fusion.12), channel_id=1, source_target_pairs={{0,12},{4,0},{8,4},{12,8},{1,13},{5,1},{9,5},{13,9},{2,14},{6,2},{... | collective-permute-start | bytes 294920 | tf_op jit(solution)/shard_map/ppermute | solution.py:27
  26.4 30.3 %collective-permute-start.22 = (bf16[192,256]{1,0:T(8,128)(2,1)S(1)}, bf16[192,256]{1,0:T(8,128)(2,1)S(1)}, u32[]{:S(2)}, u32[]{:S(2)}) collective-permute-start(bf16[192,256]{1,0:T(8,128)(2,1)S(1)} %convolution_convert_fusion.13), channel_id=1, source_target_pairs={{0,8},{4,12},{8,0},{12,4},{1,9},{5,13},{9,1},{13,5},{2,10},{6,14},... | collective-permute-start | bytes 294920 | tf_op jit(solution)/shard_map/ppermute | solution.py:27
  38.8 21.0 %copy-start.17 = (bf16[8,64,256]{2,1,0:T(8,128)(2,1)S(1)}, bf16[8,64,256]{2,1,0:T(8,128)(2,1)}, u32[]{:S(2)}) copy-start(bf16[8,64,256]{2,1,0:T(8,128)(2,1)} %param.11) | copy-start | bytes 786436
  52.2 7.6 %collective-permute-start.23 = (bf16[192,256]{1,0:T(8,128)(2,1)S(1)}, bf16[192,256]{1,0:T(8,128)(2,1)S(1)}, u32[]{:S(2)}, u32[]{:S(2)}) collective-permute-start(bf16[192,256]{1,0:T(8,128)(2,1)S(1)} %convolution_convert_fusion.14), channel_id=1, source_target_pairs={{0,4},{4,8},{8,12},{12,0},{1,5},{5,9},{9,13},{13,1},{2,6},{6,10},{... | collective-permute-start | bytes 294920 | tf_op jit(solution)/shard_map/ppermute | solution.py:27
  52.8 63.3 %collective-permute-start.18 = (bf16[192,2048]{1,0:T(8,128)(2,1)}, bf16[192,2048]{1,0:T(8,128)(2,1)}, u32[]{:S(2)}, u32[]{:S(2)}) collective-permute-start(bf16[192,2048]{1,0:T(8,128)(2,1)} %convolution_convert_fusion.11), channel_id=1, source_target_pairs={{0,12},{4,0},{8,4},{12,8},{1,13},{5,1},{9,5},{13,9},{2,14},{6,2},{... | collective-permute-start | bytes 2359304 | tf_op jit(solution)/shard_map/ppermute | solution.py:27
  56.0 104.2 %collective-permute-start.19 = (bf16[192,2048]{1,0:T(8,128)(2,1)}, bf16[192,2048]{1,0:T(8,128)(2,1)}, u32[]{:S(2)}, u32[]{:S(2)}) collective-permute-start(bf16[192,2048]{1,0:T(8,128)(2,1)} %convolution_convert_fusion.10), channel_id=1, source_target_pairs={{0,8},{4,12},{8,0},{12,4},{1,9},{5,13},{9,1},{13,5},{2,10},{6,14},... | collective-permute-start | bytes 2359304 | tf_op jit(solution)/shard_map/ppermute | solution.py:27
  56.2 104.0 %collective-permute-start.20 = (bf16[192,2048]{1,0:T(8,128)(2,1)}, bf16[192,2048]{1,0:T(8,128)(2,1)}, u32[]{:S(2)}, u32[]{:S(2)}) collective-permute-start(bf16[192,2048]{1,0:T(8,128)(2,1)} %convolution_convert_fusion.9), channel_id=1, source_target_pairs={{0,4},{4,8},{8,12},{12,0},{1,5},{5,9},{9,13},{13,1},{2,6},{6,10},{... | collective-permute-start | bytes 2359304 | tf_op jit(solution)/shard_map/ppermute | solution.py:27
  75.9 4.5 %copy-start.1 = (bf16[8,2048,64]{1,2,0:T(8,128)(2,1)S(1)}, bf16[8,2048,64]{1,2,0:T(8,128)(2,1)}, u32[]{:S(2)}) copy-start(bf16[8,2048,64]{1,2,0:T(8,128)(2,1)} %param.10) | copy-start | bytes 6291460
  81.9 114.9 %collective-permute-start.27 = (bf16[192,2048]{1,0:T(8,128)(2,1)}, bf16[192,2048]{1,0:T(8,128)(2,1)}, u32[]{:S(2)}, u32[]{:S(2)}) collective-permute-start(bf16[192,2048]{1,0:T(8,128)(2,1)} %fusion.90), channel_id=1, source_target_pairs={{0,4},{4,8},{8,12},{12,0},{1,5},{5,9},{9,13},{13,1},{2,6},{6,10},{... | collective-permute-start | bytes 2359304 | tf_op jit(solution)/shard_map/ppermute | solution.py:27
  108.4 96.2 %collective-permute-start.28 = (bf16[192,2048]{1,0:T(8,128)(2,1)}, bf16[192,2048]{1,0:T(8,128)(2,1)}, u32[]{:S(2)}, u32[]{:S(2)}) collective-permute-start(bf16[192,2048]{1,0:T(8,128)(2,1)} %fusion.91), channel_id=1, source_target_pairs={{0,8},{4,12},{8,0},{12,4},{1,9},{5,13},{9,1},{13,5},{2,10},{6,14},... | collective-permute-start | bytes 2359304 | tf_op jit(solution)/shard_map/ppermute | solution.py:27
  116.1 46.1 %copy-start.2 = (bf16[8,2048,64]{1,2,0:T(8,128)(2,1)S(1)}, bf16[8,2048,64]{1,2,0:T(8,128)(2,1)}, u32[]{:S(2)}) copy-start(bf16[8,2048,64]{1,2,0:T(8,128)(2,1)} %param.10) | copy-start | bytes 6291460
  116.1 98.2 %collective-permute-start.29 = (bf16[192,2048]{1,0:T(8,128)(2,1)}, bf16[192,2048]{1,0:T(8,128)(2,1)}, u32[]{:S(2)}, u32[]{:S(2)}) collective-permute-start(bf16[192,2048]{1,0:T(8,128)(2,1)} %fusion.92), channel_id=1, source_target_pairs={{0,12},{4,0},{8,4},{12,8},{1,13},{5,1},{9,5},{13,9},{2,14},{6,2},{... | collective-permute-start | bytes 2359304 | tf_op jit(solution)/shard_map/ppermute | solution.py:27
  162.2 3.0 %copy-start.13 = (bf16[768,2048]{1,0:T(8,128)(2,1)}, bf16[768,2048]{1,0:T(8,128)(2,1)S(1)}, u32[]{:S(2)}) copy-start(bf16[768,2048]{1,0:T(8,128)(2,1)S(1)} %pad_maximum_fusion.1) | copy-start | bytes 9437188
  182.7 0.9 copy-start.14
  188.8 30.5 %collective-permute-start.24 = (bf16[192,256]{1,0:T(8,128)(2,1)}, bf16[192,256]{1,0:T(8,128)(2,1)}, u32[]{:S(2)}, u32[]{:S(2)}) collective-permute-start(bf16[192,256]{1,0:T(8,128)(2,1)} %fusion.99), channel_id=1, source_target_pairs={{0,4},{4,8},{8,12},{12,0},{1,5},{5,9},{9,13},{13,1},{2,6},{6,10},{... | collective-permute-start | bytes 294920 | tf_op jit(solution)/shard_map/ppermute | solution.py:27
  188.8 20.1 %collective-permute-start.25 = (bf16[192,256]{1,0:T(8,128)(2,1)}, bf16[192,256]{1,0:T(8,128)(2,1)S(1)}, u32[]{:S(2)}, u32[]{:S(2)}) collective-permute-start(bf16[192,256]{1,0:T(8,128)(2,1)} %fusion.100), channel_id=1, source_target_pairs={{0,8},{4,12},{8,0},{12,4},{1,9},{5,13},{9,1},{13,5},{2,10},{6,14},... | collective-permute-start | bytes 294920 | tf_op jit(solution)/shard_map/ppermute | solution.py:27
  191.1 5.7 %copy-start.39 = (bf16[192,256]{1,0:T(8,128)(2,1)S(1)}, bf16[192,256]{1,0:T(8,128)(2,1)}, u32[]{:S(2)}) copy-start(bf16[192,256]{1,0:T(8,128)(2,1)} %fusion.101) | copy-start | bytes 294916
  196.9 7.8 %copy-start.35 = (pred[512]{0:T(512)(128)(4,1)S(1)}, pred[512]{0:T(512)(128)(4,1)}, u32[]{:S(2)}) copy-start(pred[512]{0:T(512)(128)(4,1)} %copy-done.34) | copy-start | bytes 1540
  196.9 11.6 %collective-permute-start.26 = (bf16[192,256]{1,0:T(8,128)(2,1)S(1)}, bf16[192,256]{1,0:T(8,128)(2,1)S(1)}, u32[]{:S(2)}, u32[]{:S(2)}) collective-permute-start(bf16[192,256]{1,0:T(8,128)(2,1)S(1)} %copy-done.39), channel_id=1, source_target_pairs={{0,12},{4,0},{8,4},{12,8},{1,13},{5,1},{9,5},{13,9},{2,14},{6,2},{... | collective-permute-start | bytes 294920 | tf_op jit(solution)/shard_map/ppermute | solution.py:27
  204.6 3.9 %copy-start.33 = (pred[512]{0:T(512)(128)(4,1)S(1)}, pred[512]{0:T(512)(128)(4,1)}, u32[]{:S(2)}) copy-start(pred[512]{0:T(512)(128)(4,1)} %copy-done.32) | copy-start | bytes 1540
  209.3 5.1 %copy-start.7 = (f32[512,2048]{1,0:T(8,128)S(1)}, f32[512,2048]{1,0:T(8,128)}, u32[]{:S(2)}) copy-start(f32[512,2048]{1,0:T(8,128)} %fusion.94) | copy-start | bytes 12582916
  209.3 5.1 %copy-start.8 = (f32[512,2048]{1,0:T(8,128)S(1)}, f32[512,2048]{1,0:T(8,128)}, u32[]{:S(2)}) copy-start(f32[512,2048]{1,0:T(8,128)} %fusion.109) | copy-start | bytes 12582916
  209.3 6.2 %copy-start.9 = (f32[512,2048]{1,0:T(8,128)S(1)}, f32[512,2048]{1,0:T(8,128)}, u32[]{:S(2)}) copy-start(f32[512,2048]{1,0:T(8,128)} %fusion.114) | copy-start | bytes 12582916
  219.3 1.7 copy-start.18
  219.3 1.7 copy-start.24
  219.3 1.7 copy-start.26
  221.3 2.0 copy-start.21
Sparse Core Ops, SparseCore 0:
  9.6 19.5 all-gather.4
  34.5 30.1 reduce-scatter.4

commit v3 on v2

v3 whole, which is shorter than its diff:
```python
import jax
import jax.numpy as jnp
from jax import lax
from jax.sharding import PartitionSpec as P

adapter_scale = 0.5
f32 = jnp.float32
bf16 = jnp.bfloat16


def dot(a, b, ca, cb):
    return lax.dot_general(a, b, (((ca,), (cb,)), ((), ())), preferred_element_type=f32)


def body(slots, tokens, base_weight, down, up, cotangent, ids, holder, place, fullest):
    groups = lax.axis_size("dp")
    own, width, rank = down.shape
    rows = tokens.shape[0]
    key_width = cotangent.shape[1]
    me = lax.axis_index("dp")
    down_rows = jnp.transpose(down, (0, 2, 1)).reshape(own * rank, width)
    up_rows = up.reshape(own * rank, key_width)
    code_rows = -(-own // 16) * 16

    def shifted(array, step):
        if step == 0:
            return array
        return lax.ppermute(array, "dp", [(i, (i + step) % groups) for i in range(groups)])

    def swapped(array):
        return lax.all_to_all(array, "dp", split_axis=0, concat_axis=0, tiled=True)

    seat = holder * slots + place
    seats = jnp.arange(groups * slots, dtype=jnp.int32)
    pick = ((seat[None, :] == seats[:, None]) & (place < slots)[None, :]).astype(bf16)
    local_id = jnp.arange(code_rows, dtype=jnp.int32)
    code = (lax.rem(ids, own)[:, None] == local_id[None, :]).astype(bf16)
    code = dot(code, pick, 0, 1).astype(bf16).reshape(code_rows, groups, slots)
    code = jnp.pad(jnp.transpose(code, (1, 0, 2)), ((0, 0), (0, 0), (0, key_width - slots)))
    packed = dot(pick, cotangent, 1, 0).astype(bf16).reshape(groups, slots, key_width)
    packed = jnp.concatenate([packed, code], 1)
    packed, tokens = lax.optimization_barrier((packed, tokens))
    got = swapped(packed)

    slot = jnp.arange(slots, dtype=jnp.int32)
    steps = list(range(1, groups)) + [0]
    x_out = []
    for step in steps:
        to = lax.rem(me + step, groups)
        hit = (holder[None, :] == to) & (place[None, :] == slot[:, None])
        x_out.append(dot(hit.astype(bf16), tokens, 1, 0).astype(bf16))
    x_out, tokens = lax.optimization_barrier((x_out, tokens))
    x_in = [shifted(x, step) for x, step in zip(x_out, steps)]
    sources = [lax.rem(me + groups - step, groups) for step in steps]
    frozen = lax.psum_scatter(
        dot(tokens, base_weight, 1, 0), ("mp", "sub"), scatter_dimension=1, tiled=True
    )

    got = [lax.dynamic_index_in_dim(got, source, 0, keepdims=False) for source in sources]
    g_here = jnp.concatenate([one[:slots] for one in got], 0)
    codes = jnp.concatenate([one[slots:, :slots] for one in got], 1)
    owner = jnp.arange(own * rank, dtype=jnp.int32) // rank
    mask = dot(codes, (local_id[:, None] == owner[None, :]).astype(bf16), 0, 0) > 0.5

    def fold(wide):
        return jnp.where(mask, wide, 0.0).reshape(-1, own, rank).sum(1)

    def spread(narrow):
        return jnp.where(mask, jnp.tile(narrow, (1, own)), jnp.zeros((), bf16))

    back = lax.psum(fold(dot(g_here, up_rows, 1, 1)), ("mp", "sub")).astype(bf16)
    back = spread(back)
    dx_terms = []
    for k, step in enumerate(steps):
        part = back[k * slots : (k + 1) * slots]
        dx_terms.append((adapter_scale * dot(part, down_rows, 1, 0)).astype(bf16))
    dx_terms, fullest = lax.optimization_barrier((dx_terms, fullest))
    dx_in = [shifted(t, (groups - s) % groups) for t, s in zip(dx_terms, steps)]
    fullest = lax.pmax(fullest, ("groups", "dp"))
    g_wide = lax.all_gather(cotangent, ("mp", "sub"), axis=1, tiled=True)
    dx = dot(g_wide, base_weight, 1, 1)

    x_here = jnp.concatenate(x_in, 0)
    x_here, back, dx, fullest = lax.optimization_barrier((x_here, back, dx, fullest))
    out_rank = lax.psum(fold(dot(x_here, down_rows, 1, 1)), ("mp", "sub")).astype(bf16)
    out_rank = spread(out_rank)
    out_term = (adapter_scale * dot(out_rank, up_rows, 1, 0)).astype(bf16)
    out_term = out_term.reshape(groups, slots, key_width)
    order = [lax.rem(me + 2 * groups - s - 1, groups) for s in range(groups)]
    out_term = jnp.stack(
        [lax.dynamic_index_in_dim(out_term, o, 0, keepdims=False) for o in order]
    )
    out_term = swapped(out_term).reshape(groups * slots, key_width)
    lora_out = dot(pick, out_term, 0, 0)

    down_grad = adapter_scale * dot(back, x_here, 0, 0)
    down_grad = jnp.transpose(down_grad.reshape(own, rank, width), (0, 2, 1))
    up_grad = (adapter_scale * dot(out_rank, g_here, 0, 0)).reshape(own, rank, key_width)
    for term, step in zip(dx_in, steps):
        to = lax.rem(me + step, groups)
        hit = (holder[None, :] == to) & (place[None, :] == slot[:, None])
        dx = dx + dot(hit.astype(bf16), term, 0, 0)
    out = (frozen + lora_out).astype(bf16)
    return (out, dx.astype(bf16), down_grad, up_grad), fullest


def local(tokens, base_weight, down, up, cotangent, tenant):
    groups = lax.axis_size("dp")
    own = down.shape[0]
    most = own * (2 * tokens.shape[0] // (groups * own))
    usual = min(most, -(-(most * 13) // 256) * 16)
    ids = tenant[:, 0]
    holder = ids // own
    holds = holder[:, None] == jnp.arange(groups, dtype=jnp.int32)[None, :]
    counts = jnp.cumsum(holds.astype(jnp.int32), axis=0)
    place = jnp.sum(jnp.where(holds, counts - 1, 0), axis=1)
    args = (tokens, base_weight, down, up, cotangent, ids, holder, place, jnp.max(place))
    results, fullest = body(usual, *args)
    if usual == most:
        return results
    return lax.cond(fullest >= usual, lambda r: body(most, *args)[0], lambda r: r, results)


def solution(mesh):
    rows = P(("groups", "dp"), ("mp", "sub"))
    downs = P(("groups", "dp"), ("mp", "sub"), None)
    ups = P(("groups", "dp"), None, ("mp", "sub"))
    return jax.shard_map(
        local,
        mesh=mesh,
        in_specs=(rows, P(("mp", "sub"), None), downs, ups, rows, P(("groups", "dp"), None)),
        out_specs=(rows, rows, downs, ups),
        check_vma=False,
    )
```

time: 231 us -> 255 us (1.10)
  waiting for transfers between devices: 44.9 us -> 82.4 us
  starting transfers between devices: 50.3 us -> 18.5 us
  blocking collectives: 37.8 us -> 50.9 us
  local copies, waits for them, and re-layouts: 2.01 us -> 11.2 us
  matrix products: 65 us -> 61 us
    ppermute x15 -> x6, starting transfers between devices: 50.2 us -> 7.97 us  [shifted(): lax.ppermute(array, 'dp', [(i, (i + step) % groups) for i in range(groups)])]
    all_to_all x0 -> x2, waiting for transfers between devices: none -> 38.6 us  [swapped(): return lax.all_to_all(array, 'dp', split_axis=0, concat_axis=0, tiled=True)]
    pmax x1, blocking collectives: 10.6 us -> 23.9 us  [body(): fullest = lax.pmax(fullest, ('groups', 'dp'))]
    all_to_all x0 -> x2, starting transfers between devices: none -> 10.4 us  [swapped(): return lax.all_to_all(array, 'dp', split_axis=0, concat_axis=0, tiled=True)]
    select_n x0 -> x2, local copies, waits for them, and re-layouts: none -> 5.39 us  [fold(): return jnp.where(mask, wide, 0.0).reshape(-1, own, rank).sum(1)]
    another operation x0 -> x4, local copies, waits for them, and re-layouts: none -> 4.59 us  [spread(): return jnp.where(mask, jnp.tile(narrow, (1, own)), jnp.zeros((), bf16))]
    dot_general x28 -> x23, matrix products: 65 us -> 61 us  [dot(): lax.dot_general(a, b, (((ca,), (cb,)), ((), ())), preferred_element_type=...]
    ppermute x15 -> x6, waiting for transfers between devices: 44.1 us -> 43.1 us  [shifted(): lax.ppermute(array, 'dp', [(i, (i + step) % groups) for i in range(groups)])]
  transfers between devices with their start and end apart: 17 -> 10, of which waited for: 2 -> 2; matrix products, arithmetic and copies ran while one was open for 33% -> 33% of each run, Pallas kernels for 0% -> 0%
where the time goes in v3:
time: 255 us
  waiting for transfers between devices  82.4 us (32%)
  matrix products  61 us (24%)
  blocking collectives  50.9 us (20%)
  starting transfers between devices  18.5 us (7%)
  other arithmetic  15.2 us (6%)
  between operations  15.1 us (6%)
  local copies, waits for them, and re-layouts  11.2 us (4%)
    dot_general x23, matrix products, dot(): lax.dot_general(a, b, (((ca,), (cb,)), ((), ())), preferred_element_type=...  61 us
    ppermute x6, waiting for transfers between devices, shifted(): lax.ppermute(array, 'dp', [(i, (i + step) % groups) for i in range(groups)])  43.1 us
    all_to_all x2, waiting for transfers between devices, swapped(): return lax.all_to_all(array, 'dp', split_axis=0, concat_axis=0, tiled=True)  38.6 us
    pmax x1, blocking collectives, body(): fullest = lax.pmax(fullest, ('groups', 'dp'))  23.9 us
    psum x1, blocking collectives, body(): lax.psum(fold(dot(x_here, down_rows, 1, 1)), ('mp', 'sub')).astype(bf16)  13.6 us
    psum x1, blocking collectives, body(): lax.psum(fold(dot(g_here, up_rows, 1, 1)), ('mp', 'sub')).astype(bf16)  13.4 us
    all_to_all x2, starting transfers between devices, swapped(): return lax.all_to_all(array, 'dp', split_axis=0, concat_axis=0, tiled=True)  10.4 us
    ppermute x6, starting transfers between devices, shifted(): lax.ppermute(array, 'dp', [(i, (i + step) % groups) for i in range(groups)])  7.97 us
  transfers between devices with their start and end apart: 10, of which 2 were waited for; matrix products, arithmetic and copies ran while one was open for 33% of the time, Pallas kernels for 0%

profile of v3, /device:TPU:0, one launch (start us, length us, event | category | flops | bytes accessed | tf_op | source)
XLA Modules:
  0.0 254.5 jit_solution(9537522206551152459)
XLA Ops:
  7.2 0.7 all-gather.5.cloned.1.call-update
  7.9 0.7 and_select_fusion
  8.6 1.2 reduce-window.6
  10.4 0.7 broadcast_compare_fusion.5
  11.7 1.6 fusion.99
  13.9 0.8 fusion.121
  14.7 6.3 %all-to-all-start.2 = ((bf16[4,224,256]{2,1,0:T(8,128)(2,1)}), bf16[4,224,256]{2,1,0:T(8,128)(2,1)S(1)}, u32[]{:S(2)}, u32[]{:S(2)}) async-start(bf16[4,224,256]{2,1,0:T(8,128)(2,1)} %fusion.121), calls=%async_computation.3 | async-start | bytes 917504 | tf_op jit(solution)/shard_map/all_to_all | solution.py:31
  21.0 1.5 convolution_convert_fusion.5
  22.6 1.5 convolution_convert_fusion.6
  24.1 1.5 convolution_convert_fusion.4
  25.6 1.6 convolution_convert_fusion.7
  27.2 2.0 collective-permute-start.6
  29.2 2.4 collective-permute-start.7
  31.6 1.4 collective-permute-start.8
  33.0 38.6 %all-to-all-done.2 = bf16[4,224,256]{2,1,0:T(8,128)(2,1)S(1)} async-done(((bf16[4,224,256]{2,1,0:T(8,128)(2,1)}), bf16[4,224,256]{2,1,0:T(8,128)(2,1)S(1)}, u32[]{:S(2)}, u32[]{:S(2)}) %all-to-all-start.2) | async-done | bytes 458784 | tf_op jit(solution)/shard_map/all_to_all | solution.py:31
  72.7 1.6 convolution_select_fusion.2
  74.3 2.7 %copy.15 = f32[832,512]{0,1:T(8,128)} copy(f32[832,512]{1,0:T(8,128)} %convolution_select_fusion.2) | data formatting | bytes 3407872 | tf_op jit(solution)/shard_map/jit(_where)/select_n | solution.py:66
  77.0 1.6 reduce_sum.46
  78.6 13.4 %all-reduce.7 = bf16[832,64]{0,1:T(8,128)(2,1)S(1)} all-reduce(f32[832,64]{0,1:T(8,128)S(1)} %reduce_sum.46), channel_id=1, replica_groups=mesh['groups'=2,'dp'=4,'mp'=2,'sub'=2] {'mp','sub'}, use_global_device_ids=true, to_apply=%region_4.5 | all-reduce | flops 53248 | bytes 319488 | tf_op jit(solution)/shard_map/psum | solution.py:71
  92.2 1.2 copy.16
  93.5 1.6 broadcast_select_fusion
  95.4 1.5 fusion.87
  97.0 1.5 fusion.88
  98.5 1.5 fusion.89
  100.0 1.5 fusion.90
  101.6 3.7 %fusion.190 = f32[512,1024]{1,0:T(8,128)} fusion(bf16[512,2048]{1,0:T(8,128)(2,1)S(1)} %copy-done, bf16[2048,1024]{1,0:T(8,128)(2,1)S(1)} %copy-done.41), kind=kOutput, calls=%fused_computation.256 | convolution fusion | flops 2147483648 | bytes 8388608 | tf_op jit(solution)/shard_map/dot_general | solution.py:12
  105.3 23.9 %pmax.6 = s32[]{:T(128)} all-reduce(s32[]{:T(128)} %get-tuple-element.85), channel_id=1, replica_groups=mesh['groups'=2,'dp'=4,'mp'=2,'sub'=2] {'groups','dp'}, use_global_device_ids=true, to_apply=%region_6.7 | all-reduce | flops 1 | bytes 8 | tf_op jit(solution)/shard_map/pmax | solution.py:79
  129.2 1.8 collective-permute-start.10
  131.1 3.9 %fusion.139 = f32[512,2048]{1,0:T(8,128)} fusion(bf16[208,2048]{1,0:T(8,128)(2,1)} %fusion.90, s32[512]{0:T(512)S(1)} %fusion.174, pred[512]{0:T(512)(128)(4,1)S(1)} %get-tuple-element.107), kind=kOutput, calls=%fused_computation.168 | convolution fusion | flops 436420608 | bytes 5048832 | tf_op jit(solution)/shard_map/dot_general | solution.py:12
  135.3 3.2 %pad_maximum_fusion.6 = bf16[832,2048]{1,0:T(8,128)(2,1)} fusion(bf16[208,2048]{1,0:T(8,128)(2,1)S(1)} %copy-done.10, bf16[208,2048]{1,0:T(8,128)(2,1)} %collective-permute-done.8, bf16[208,2048]{1,0:T(8,128)(2,1)} %collective-permute-done.7, bf16[208,2048]{1,0:T(8,128)(2,1)} %collective-permute-done.6), kind=kLoop, calls=%fused_computation.115 | loop fusion | flops 13631488 | bytes 6815744 | tf_op jit(solution)/shard_map/concatenate | solution.py:83
  138.5 3.9 %fusion.128 = f32[512,2048]{1,0:T(8,128)} fusion(bf16[208,2048]{1,0:T(8,128)(2,1)} %collective-permute-done.9, s32[512]{0:T(512)S(1)} %fusion.174, pred[512]{0:T(512)(128)(4,1)S(1)} %get-tuple-element.145), kind=kOutput, calls=%fused_computation.165 | convolution fusion | flops 436420608 | bytes 5048832 | tf_op jit(solution)/shard_map/dot_general | solution.py:12
  142.4 43.1 %collective-permute-done.10 = bf16[208,2048]{1,0:T(8,128)(2,1)S(1)} collective-permute-done((bf16[208,2048]{1,0:T(8,128)(2,1)}, bf16[208,2048]{1,0:T(8,128)(2,1)S(1)}, u32[]{:S(2)}, u32[]{:S(2)}) %collective-permute-start.10) | collective-permute-done | bytes 852000 | tf_op jit(solution)/shard_map/ppermute | solution.py:28
  185.5 2.8 %fusion.131 = f32[512,2048]{1,0:T(8,128)} fusion(bf16[208,2048]{1,0:T(8,128)(2,1)S(1)} %collective-permute-done.10, s32[512]{0:T(512)S(1)} %fusion.174, pred[512]{0:T(512)(128)(4,1)S(1)} %get-tuple-element.144), kind=kOutput, calls=%fused_computation.166 | convolution fusion | flops 436420608 | bytes 5048832 | tf_op jit(solution)/shard_map/dot_general | solution.py:12
  188.3 7.1 %fusion.189 = f32[512,2048]{1,0:T(8,128)} fusion(bf16[512,1024]{1,0:T(8,128)(2,1)} %all-gather.5.cloned.1.call-done, bf16[2048,1024]{1,0:T(8,128)(2,1)} %param.9), kind=kOutput, calls=%fused_computation.255 | convolution fusion | flops 2147483648 | bytes 9437184 | tf_op jit(solution)/shard_map/dot_general | solution.py:12
  195.4 3.2 %convolution_select_fusion.3 = f32[832,512]{1,0:T(8,128)} fusion(pred[832,512]{1,0:T(32,128)(4,1)S(1)} %copy-done.16, bf16[832,2048]{1,0:T(8,128)(2,1)S(1)} %copy-done.5, bf16[512,2048]{1,0:T(8,128)(2,1)S(1)} %bitcast.146), kind=kOutput, calls=%fused_computation.135 | convolution fusion | flops 1745256448 | bytes 7634944 | tf_op jit(solution)/shard_map/dot_general | solution.py:12
  198.5 2.7 %copy.17 = f32[832,512]{0,1:T(8,128)} copy(f32[832,512]{1,0:T(8,128)} %convolution_select_fusion.3) | data formatting | bytes 3407872 | tf_op jit(solution)/shard_map/jit(_where)/select_n | solution.py:66
  201.2 1.6 reduce_sum.47
  202.9 13.6 %all-reduce.8 = bf16[832,64]{0,1:T(8,128)(2,1)S(1)} all-reduce(f32[832,64]{0,1:T(8,128)S(1)} %reduce_sum.47), channel_id=1, replica_groups=mesh['groups'=2,'dp'=4,'mp'=2,'sub'=2] {'mp','sub'}, use_global_device_ids=true, to_apply=%region_9.10 | all-reduce | flops 53248 | bytes 319488 | tf_op jit(solution)/shard_map/psum | solution.py:85
  216.4 1.0 tile.18
  217.5 2.2 copy.18
  219.7 1.8 fusion.98
  221.5 0.8 pad_maximum_fusion.8
  222.3 4.1 %all-to-all-start.3 = ((bf16[4,208,256]{2,1,0:T(8,128)(2,1)}), bf16[4,208,256]{2,1,0:T(8,128)(2,1)}, u32[]{:S(2)}, u32[]{:S(2)}) async-start(bf16[4,208,256]{2,1,0:T(8,128)(2,1)} %pad_maximum_fusion.8), calls=%async_computation.5 | async-start | bytes 851968 | tf_op jit(solution)/shard_map/all_to_all | solution.py:31
  226.5 8.6 %add_convert_fusion.1 = bf16[512,2048]{1,0:T(8,128)(2,1)} fusion(f32[512,2048]{1,0:T(8,128)} %fusion.139, f32[512,2048]{1,0:T(8,128)} %fusion.131, f32[512,2048]{1,0:T(8,128)} %fusion.189, f32[512,2048]{1,0:T(8,128)} %fusion.128, bf16[208,2048]{1,0:T(8,128)(2,1)} %collective-permute-done.11, s32[512]{0:T(512)S(1)} %fusion.174, ...), kind=kOutput, calls=%fused_computation.114 | convolution fusion | flops 441663488 | bytes 19728896 | tf_op jit(solution)/shard_map/dot_general | solution.py:12
  235.2 1.3 fusion.119
  237.1 6.4 %convolution_multiply_fusion.6 = f32[512,2048]{1,0:T(8,128)} fusion(bf16[832,512]{1,0:T(8,128)(2,1)S(1)} %broadcast_select_fusion, bf16[832,2048]{1,0:T(8,128)(2,1)} %pad_maximum_fusion.6), kind=kOutput, calls=%fused_computation.116 | convolution fusion | flops 1745879040 | bytes 8454144 | tf_op jit(solution)/shard_map/dot_general | solution.py:12
  243.5 1.8 fusion.105
  245.7 2.0 broadcast_multiply_fusion
  (75 shorter events, 3.9 us)
Async XLA Ops:
  7.2 181.1 %all-gather.5.cloned.1.call-start = ((), (), s32[]{:S(2)}) async-start(), calls=%async_computation.8 | async-start | bytes 1310720 | tf_op jit(solution)/shard_map/all_gather | solution.py:80
  11.7 9.3 %copy-start = (bf16[512,2048]{1,0:T(8,128)(2,1)S(1)}, bf16[512,2048]{1,0:T(8,128)(2,1)}, u32[]{:S(2)}) copy-start(bf16[512,2048]{1,0:T(8,128)(2,1)} %param.8) | copy-start | bytes 6291460
  14.7 57.0 %all-to-all-start.2 = ((bf16[4,224,256]{2,1,0:T(8,128)(2,1)}), bf16[4,224,256]{2,1,0:T(8,128)(2,1)S(1)}, u32[]{:S(2)}, u32[]{:S(2)}) async-start(bf16[4,224,256]{2,1,0:T(8,128)(2,1)} %fusion.121), calls=%async_computation.3 | async-start | bytes 917504 | tf_op jit(solution)/shard_map/all_to_all | solution.py:31
  21.0 222.5 %reduce-scatter.5.cloned.1.call-start = ((), (), s32[]{:S(2)}) async-start(), calls=%async_computation.9 | async-start | bytes 2621440 | tf_op jit(solution)/shard_map/reduce_scatter | solution.py:55
  27.2 107.8 %collective-permute-start.6 = (bf16[208,2048]{1,0:T(8,128)(2,1)}, bf16[208,2048]{1,0:T(8,128)(2,1)}, u32[]{:S(2)}, u32[]{:S(2)}) collective-permute-start(bf16[208,2048]{1,0:T(8,128)(2,1)} %convolution_convert_fusion.7), channel_id=1, source_target_pairs={{0,4},{4,8},{8,12},{12,0},{1,5},{5,9},{9,13},{13,1},{2,6},{6,10},{... | collective-permute-start | bytes 2555912 | tf_op jit(solution)/shard_map/ppermute | solution.py:28
  29.2 106.1 %collective-permute-start.7 = (bf16[208,2048]{1,0:T(8,128)(2,1)}, bf16[208,2048]{1,0:T(8,128)(2,1)}, u32[]{:S(2)}, u32[]{:S(2)}) collective-permute-start(bf16[208,2048]{1,0:T(8,128)(2,1)} %convolution_convert_fusion.6), channel_id=1, source_target_pairs={{0,8},{4,12},{8,0},{12,4},{1,9},{5,13},{9,1},{13,5},{2,10},{6,14},... | collective-permute-start | bytes 2555912 | tf_op jit(solution)/shard_map/ppermute | solution.py:28
  31.6 103.7 %collective-permute-start.8 = (bf16[208,2048]{1,0:T(8,128)(2,1)}, bf16[208,2048]{1,0:T(8,128)(2,1)}, u32[]{:S(2)}, u32[]{:S(2)}) collective-permute-start(bf16[208,2048]{1,0:T(8,128)(2,1)} %convolution_convert_fusion.5), channel_id=1, source_target_pairs={{0,12},{4,0},{8,4},{12,8},{1,13},{5,1},{9,5},{13,9},{2,14},{6,2},{... | collective-permute-start | bytes 2555912 | tf_op jit(solution)/shard_map/ppermute | solution.py:28
  71.7 1.0 copy-start.43
  72.3 4.7 %copy-start.15 = (pred[832,512]{1,0:T(32,128)(4,1)}, pred[832,512]{1,0:T(32,128)(4,1)S(1)}, u32[]{:S(2)}) copy-start(pred[832,512]{1,0:T(32,128)(4,1)S(1)} %convolution_compare_fusion.1) | copy-start | bytes 1277956
  72.3 4.7 %copy-start.26 = (bf16[208,256]{1,0:T(8,128)(2,1)}, bf16[208,256]{1,0:T(8,128)(2,1)S(1)}, u32[]{:S(2)}) copy-start(bf16[208,256]{1,0:T(8,128)(2,1)S(1)} %get-tuple-element.130) | copy-start | bytes 319492
  72.4 4.7 %copy-start.28 = (bf16[208,256]{1,0:T(8,128)(2,1)}, bf16[208,256]{1,0:T(8,128)(2,1)S(1)}, u32[]{:S(2)}) copy-start(bf16[208,256]{1,0:T(8,128)(2,1)S(1)} %get-tuple-element.131) | copy-start | bytes 319492
  72.4 4.7 %copy-start.30 = (bf16[208,256]{1,0:T(8,128)(2,1)}, bf16[208,256]{1,0:T(8,128)(2,1)S(1)}, u32[]{:S(2)}) copy-start(bf16[208,256]{1,0:T(8,128)(2,1)S(1)} %get-tuple-element.132) | copy-start | bytes 319492
  93.5 2.0 copy-start.1
  98.5 3.0 %copy-start.41 = (bf16[2048,1024]{1,0:T(8,128)(2,1)S(1)}, bf16[2048,1024]{1,0:T(8,128)(2,1)}, u32[]{:S(2)}) copy-start(bf16[2048,1024]{1,0:T(8,128)(2,1)} %param.9) | copy-start | bytes 12582916
  101.6 37.0 %collective-permute-start.9 = (bf16[208,2048]{1,0:T(8,128)(2,1)}, bf16[208,2048]{1,0:T(8,128)(2,1)}, u32[]{:S(2)}, u32[]{:S(2)}) collective-permute-start(bf16[208,2048]{1,0:T(8,128)(2,1)} %fusion.87), channel_id=1, source_target_pairs={{0,12},{4,0},{8,4},{12,8},{1,13},{5,1},{9,5},{13,9},{2,14},{6,2},{... | collective-permute-start | bytes 2555912 | tf_op jit(solution)/shard_map/ppermute | solution.py:28
  129.2 6.1 %copy-start.10 = (bf16[208,2048]{1,0:T(8,128)(2,1)S(1)}, bf16[208,2048]{1,0:T(8,128)(2,1)}, u32[]{:S(2)}) copy-start(bf16[208,2048]{1,0:T(8,128)(2,1)} %convolution_convert_fusion.4) | copy-start | bytes 2555908
  129.2 56.3 %collective-permute-start.10 = (bf16[208,2048]{1,0:T(8,128)(2,1)}, bf16[208,2048]{1,0:T(8,128)(2,1)S(1)}, u32[]{:S(2)}, u32[]{:S(2)}) collective-permute-start(bf16[208,2048]{1,0:T(8,128)(2,1)} %fusion.88), channel_id=1, source_target_pairs={{0,8},{4,12},{8,0},{12,4},{1,9},{5,13},{9,1},{13,5},{2,10},{6,14},... | collective-permute-start | bytes 2555912 | tf_op jit(solution)/shard_map/ppermute | solution.py:28
  135.0 91.5 %collective-permute-start.11 = (bf16[208,2048]{1,0:T(8,128)(2,1)}, bf16[208,2048]{1,0:T(8,128)(2,1)}, u32[]{:S(2)}, u32[]{:S(2)}) collective-permute-start(bf16[208,2048]{1,0:T(8,128)(2,1)} %fusion.89), channel_id=1, source_target_pairs={{0,4},{4,8},{8,12},{12,0},{1,5},{5,9},{9,13},{13,1},{2,6},{6,10},{... | collective-permute-start | bytes 2555912 | tf_op jit(solution)/shard_map/ppermute | solution.py:28
  188.3 7.1 %copy-start.2 = (bf16[8,2048,64]{1,2,0:T(8,128)(2,1)S(1)}, bf16[8,2048,64]{1,2,0:T(8,128)(2,1)}, u32[]{:S(2)}) copy-start(bf16[8,2048,64]{1,2,0:T(8,128)(2,1)} %param.10) | copy-start | bytes 6291460
  188.3 7.1 %copy-start.5 = (bf16[832,2048]{1,0:T(8,128)(2,1)S(1)}, bf16[832,2048]{1,0:T(8,128)(2,1)}, u32[]{:S(2)}) copy-start(bf16[832,2048]{1,0:T(8,128)(2,1)} %pad_maximum_fusion.6) | copy-start | bytes 10223620
  188.3 7.1 %copy-start.16 = (pred[832,512]{1,0:T(32,128)(4,1)S(1)}, pred[832,512]{1,0:T(32,128)(4,1)}, u32[]{:S(2)}) copy-start(pred[832,512]{1,0:T(32,128)(4,1)} %copy-done.15) | copy-start | bytes 1277956
  222.3 21.2 %all-to-all-start.3 = ((bf16[4,208,256]{2,1,0:T(8,128)(2,1)}), bf16[4,208,256]{2,1,0:T(8,128)(2,1)}, u32[]{:S(2)}, u32[]{:S(2)}) async-start(bf16[4,208,256]{2,1,0:T(8,128)(2,1)} %pad_maximum_fusion.8), calls=%async_computation.5 | async-start | bytes 851968 | tf_op jit(solution)/shard_map/all_to_all | solution.py:31
  226.4 8.7 %copy-start.14 = (bf16[832,512]{1,0:T(8,128)(2,1)S(1)}, bf16[832,512]{1,0:T(8,128)(2,1)}, u32[]{:S(2)}) copy-start(bf16[832,512]{1,0:T(8,128)(2,1)} %copy.18) | copy-start | bytes 2555908
  226.4 8.7 %copy-start.17 = (pred[832,512]{1,0:T(32,128)(4,1)S(1)}, pred[832,512]{1,0:T(32,128)(4,1)}, u32[]{:S(2)}) copy-start(pred[832,512]{1,0:T(32,128)(4,1)} %copy-done.15) | copy-start | bytes 1277956
  226.5 8.7 %copy-start.27 = (bf16[208,256]{1,0:T(8,128)(2,1)S(1)}, bf16[208,256]{1,0:T(8,128)(2,1)}, u32[]{:S(2)}) copy-start(bf16[208,256]{1,0:T(8,128)(2,1)} %copy-done.26) | copy-start | bytes 319492
  226.5 8.7 %copy-start.29 = (bf16[208,256]{1,0:T(8,128)(2,1)S(1)}, bf16[208,256]{1,0:T(8,128)(2,1)}, u32[]{:S(2)}) copy-start(bf16[208,256]{1,0:T(8,128)(2,1)} %copy-done.28) | copy-start | bytes 319492
  226.5 8.7 %copy-start.31 = (bf16[208,256]{1,0:T(8,128)(2,1)S(1)}, bf16[208,256]{1,0:T(8,128)(2,1)}, u32[]{:S(2)}) copy-start(bf16[208,256]{1,0:T(8,128)(2,1)} %copy-done.30) | copy-start | bytes 319492
  237.1 8.3 %copy-start.34 = (s32[512,1]{0,1:T(1,128)S(1)}, s32[512,1]{0,1:T(1,128)}, u32[]{:S(2)}) copy-start(s32[512,1]{0,1:T(1,128)} %param.13) | copy-start | bytes 6148
  237.1 8.3 %copy-start.44 = (bf16[8,64,256]{2,1,0:T(8,128)(2,1)S(1)}, bf16[8,64,256]{2,1,0:T(8,128)(2,1)}, u32[]{:S(2)}) copy-start(bf16[8,64,256]{2,1,0:T(8,128)(2,1)} %param.11) | copy-start | bytes 786436
  245.7 2.0 copy-start.47
Sparse Core Ops, SparseCore 0:
  9.6 19.5 all-gather.4
  105.4 31.0 reduce-scatter.4

commit v4 on v3

--- a/solution.py
+++ b/solution.py
@@ -21,6 +21,7 @@
     down_rows = jnp.transpose(down, (0, 2, 1)).reshape(own * rank, width)
     up_rows = up.reshape(own * rank, key_width)
     code_rows = -(-own // 16) * 16
+    g_wide = lax.all_gather(cotangent, ("mp", "sub"), axis=1, tiled=True)
 
     def shifted(array, step):
         if step == 0:
@@ -49,12 +50,9 @@
         to = lax.rem(me + step, groups)
         hit = (holder[None, :] == to) & (place[None, :] == slot[:, None])
         x_out.append(dot(hit.astype(bf16), tokens, 1, 0).astype(bf16))
-    x_out, tokens = lax.optimization_barrier((x_out, tokens))
+    x_out, got, tokens = lax.optimization_barrier((x_out, got, tokens))
     x_in = [shifted(x, step) for x, step in zip(x_out, steps)]
     sources = [lax.rem(me + groups - step, groups) for step in steps]
-    frozen = lax.psum_scatter(
-        dot(tokens, base_weight, 1, 0), ("mp", "sub"), scatter_dimension=1, tiled=True
-    )
 
     got = [lax.dynamic_index_in_dim(got, source, 0, keepdims=False) for source in sources]
     g_here = jnp.concatenate([one[:slots] for one in got], 0)
@@ -74,14 +72,15 @@
     for k, step in enumerate(steps):
         part = back[k * slots : (k + 1) * slots]
         dx_terms.append((adapter_scale * dot(part, down_rows, 1, 0)).astype(bf16))
-    dx_terms, fullest = lax.optimization_barrier((dx_terms, fullest))
+    dx_terms, tokens, g_wide = lax.optimization_barrier((dx_terms, tokens, g_wide))
+    frozen = dot(tokens, base_weight, 1, 0)
+    dx = dot(g_wide, base_weight, 1, 1)
+    frozen, dx, dx_terms = lax.optimization_barrier((frozen, dx, dx_terms))
+    frozen = lax.psum_scatter(frozen, ("mp", "sub"), scatter_dimension=1, tiled=True)
     dx_in = [shifted(t, (groups - s) % groups) for t, s in zip(dx_terms, steps)]
-    fullest = lax.pmax(fullest, ("groups", "dp"))
-    g_wide = lax.all_gather(cotangent, ("mp", "sub"), axis=1, tiled=True)
-    dx = dot(g_wide, base_weight, 1, 1)
 
     x_here = jnp.concatenate(x_in, 0)
-    x_here, back, dx, fullest = lax.optimization_barrier((x_here, back, dx, fullest))
+    x_here, back, dx = lax.optimization_barrier((x_here, back, dx))
     out_rank = lax.psum(fold(dot(x_here, down_rows, 1, 1)), ("mp", "sub")).astype(bf16)
     out_rank = spread(out_rank)
     out_term = (adapter_scale * dot(out_rank, up_rows, 1, 0)).astype(bf16)
@@ -90,12 +89,15 @@
     out_term = jnp.stack(
         [lax.dynamic_index_in_dim(out_term, o, 0, keepdims=False) for o in order]
     )
+    out_term, fullest = lax.optimization_barrier((out_term, fullest))
     out_term = swapped(out_term).reshape(groups * slots, key_width)
+    fullest = lax.pmax(fullest, ("groups", "dp"))
     lora_out = dot(pick, out_term, 0, 0)
 
     down_grad = adapter_scale * dot(back, x_here, 0, 0)
     down_grad = jnp.transpose(down_grad.reshape(own, rank, width), (0, 2, 1))
     up_grad = (adapter_scale * dot(out_rank, g_here, 0, 0)).reshape(own, rank, key_width)
+    down_grad, up_grad, dx, fullest = lax.optimization_barrier((down_grad, up_grad, dx, fullest))
     for term, step in zip(dx_in, steps):
         to = lax.rem(me + step, groups)
         hit = (holder[None, :] == to) & (place[None, :] == slot[:, None])

time: 255 us -> 219 us (0.86)
  waiting for transfers between devices: 82.4 us -> 22.7 us
  blocking collectives: 50.9 us -> 70.6 us
  starting transfers between devices: 18.5 us -> 33.7 us
  matrix products: 61 us -> 51.6 us
  other arithmetic: 15.2 us -> 12.2 us
    all_to_all x2, waiting for transfers between devices: 38.6 us -> 8.17 us  [swapped(): return lax.all_to_all(array, 'dp', split_axis=0, concat_axis=0, tiled=True)]
    ppermute x6, waiting for transfers between devices: 43.1 us -> 13.8 us  [shifted(): lax.ppermute(array, 'dp', [(i, (i + step) % groups) for i in range(groups)])]
    pmax x1, blocking collectives: 23.9 us -> 43.9 us  [body(): fullest = lax.pmax(fullest, ('groups', 'dp'))]
    ppermute x6, starting transfers between devices: 7.97 us -> 23.2 us  [shifted(): lax.ppermute(array, 'dp', [(i, (i + step) % groups) for i in range(groups)])]
    dot_general x23, matrix products: 61 us -> 51.6 us  [dot(): lax.dot_general(a, b, (((ca,), (cb,)), ((), ())), preferred_element_type=...]
  transfers between devices with their start and end apart: 10 -> 10, of which waited for: 2 -> 3; matrix products, arithmetic and copies ran while one was open for 33% -> 33% of each run, Pallas kernels for 0% -> 0%
where the time goes in v4:
time: 219 us
  blocking collectives  70.6 us (32%)
  matrix products  51.6 us (24%)
  starting transfers between devices  33.7 us (15%)
  waiting for transfers between devices  22.7 us (10%)
  between operations  15.1 us (7%)
  local copies, waits for them, and re-layouts  12.6 us (6%)
  other arithmetic  12.2 us (6%)
    dot_general x23, matrix products, dot(): lax.dot_general(a, b, (((ca,), (cb,)), ((), ())), preferred_element_type=...  51.6 us
    pmax x1, blocking collectives, body(): fullest = lax.pmax(fullest, ('groups', 'dp'))  43.9 us
    ppermute x6, starting transfers between devices, shifted(): lax.ppermute(array, 'dp', [(i, (i + step) % groups) for i in range(groups)])  23.2 us
    ppermute x6, waiting for transfers between devices, shifted(): lax.ppermute(array, 'dp', [(i, (i + step) % groups) for i in range(groups)])  13.8 us
    psum x1, blocking collectives, body(): lax.psum(fold(dot(g_here, up_rows, 1, 1)), ('mp', 'sub')).astype(bf16)  13.6 us
    psum x1, blocking collectives, body(): lax.psum(fold(dot(x_here, down_rows, 1, 1)), ('mp', 'sub')).astype(bf16)  13.1 us
    all_to_all x2, starting transfers between devices, swapped(): return lax.all_to_all(array, 'dp', split_axis=0, concat_axis=0, tiled=True)  10.4 us
    all_to_all x2, waiting for transfers between devices, swapped(): return lax.all_to_all(array, 'dp', split_axis=0, concat_axis=0, tiled=True)  8.17 us
  transfers between devices with their start and end apart: 10, of which 3 were waited for; matrix products, arithmetic and copies ran while one was open for 33% of the time, Pallas kernels for 0%

profile of v4, /device:TPU:0, one launch (start us, length us, event | category | flops | bytes accessed | tf_op | source)
XLA Modules:
  0.0 218.8 jit_solution(10302597129847371792)
XLA Ops:
  7.9 0.7 and_select_fusion
  8.6 1.2 reduce-window.6
  10.4 0.7 broadcast_compare_fusion.5
  11.7 1.6 fusion.98
  13.9 0.8 fusion.119
  14.7 6.3 %all-to-all-start.2 = ((bf16[4,224,256]{2,1,0:T(8,128)(2,1)}), bf16[4,224,256]{2,1,0:T(8,128)(2,1)S(1)}, u32[]{:S(2)}, u32[]{:S(2)}) async-start(bf16[4,224,256]{2,1,0:T(8,128)(2,1)} %fusion.119), calls=%async_computation.3 | async-start | bytes 917504 | tf_op jit(solution)/shard_map/all_to_all | solution.py:32
  21.0 1.5 convolution_convert_fusion.4
  22.6 1.5 convolution_convert_fusion.5
  24.1 1.5 convolution_convert_fusion.6
  25.6 1.5 convolution_convert_fusion.7
  27.2 6.9 %all-to-all-done.2 = bf16[4,224,256]{2,1,0:T(8,128)(2,1)S(1)} async-done(((bf16[4,224,256]{2,1,0:T(8,128)(2,1)}), bf16[4,224,256]{2,1,0:T(8,128)(2,1)S(1)}, u32[]{:S(2)}, u32[]{:S(2)}) %all-to-all-start.2) | async-done | bytes 458784 | tf_op jit(solution)/shard_map/all_to_all | solution.py:32
  34.3 2.0 collective-permute-start.7
  36.4 1.8 collective-permute-start.8
  38.7 0.7 copy-done.16
  39.4 1.6 convolution_select_fusion.2
  41.0 2.7 %copy.23 = f32[832,512]{0,1:T(8,128)} copy(f32[832,512]{1,0:T(8,128)} %convolution_select_fusion.2) | data formatting | bytes 3407872 | tf_op jit(solution)/shard_map/jit(_where)/select_n | solution.py:64
  43.7 1.6 reduce_sum.46
  45.4 13.6 %all-reduce.7 = bf16[832,64]{0,1:T(8,128)(2,1)S(1)} all-reduce(f32[832,64]{0,1:T(8,128)S(1)} %reduce_sum.46), channel_id=1, replica_groups=mesh['groups'=2,'dp'=4,'mp'=2,'sub'=2] {'mp','sub'}, use_global_device_ids=true, to_apply=%region_4.5 | all-reduce | flops 53248 | bytes 319488 | tf_op jit(solution)/shard_map/psum | solution.py:69
  59.1 1.2 copy.24
  60.4 1.6 broadcast_select_fusion
  62.3 1.5 fusion.89
  63.9 1.5 fusion.88
  65.4 1.6 fusion.87
  67.0 1.5 fusion.86
  68.5 7.0 %fusion.188 = f32[512,2048]{1,0:T(8,128)} fusion(bf16[512,1024]{1,0:T(8,128)(2,1)} %all-gather.5.cloned.1.call-done, bf16[2048,1024]{1,0:T(8,128)(2,1)} %param.9), kind=kOutput, calls=%fused_computation.255 | convolution fusion | flops 2147483648 | bytes 9437184 | tf_op jit(solution)/shard_map/dot_general | solution.py:12
  75.5 3.7 %fusion.187 = f32[512,1024]{1,0:T(8,128)} fusion(bf16[512,2048]{1,0:T(8,128)(2,1)S(1)} %copy-done, bf16[2048,1024]{1,0:T(8,128)(2,1)S(1)} %copy-done.35), kind=kOutput, calls=%fused_computation.254 | convolution fusion | flops 2147483648 | bytes 8388608 | tf_op jit(solution)/shard_map/dot_general | solution.py:12
  79.3 13.8 %collective-permute-done.7 = bf16[208,2048]{1,0:T(8,128)(2,1)} collective-permute-done((bf16[208,2048]{1,0:T(8,128)(2,1)}, bf16[208,2048]{1,0:T(8,128)(2,1)}, u32[]{:S(2)}, u32[]{:S(2)}) %collective-permute-start.7) | collective-permute-done | bytes 852000 | tf_op jit(solution)/shard_map/ppermute | solution.py:29
  93.1 2.1 pad_maximum_fusion.6
  95.2 16.7 %collective-permute-start.9 = (bf16[208,2048]{1,0:T(8,128)(2,1)}, bf16[208,2048]{1,0:T(8,128)(2,1)}, u32[]{:S(2)}, u32[]{:S(2)}) collective-permute-start(bf16[208,2048]{1,0:T(8,128)(2,1)} %fusion.86), channel_id=1, source_target_pairs={{0,12},{4,0},{8,4},{12,8},{1,13},{5,1},{9,5},{13,9},{2,14},{6,2},{... | collective-permute-start | bytes 2555912 | tf_op jit(solution)/shard_map/ppermute | solution.py:29
  111.9 2.7 %collective-permute-start.10 = (bf16[208,2048]{1,0:T(8,128)(2,1)}, bf16[208,2048]{1,0:T(8,128)(2,1)}, u32[]{:S(2)}, u32[]{:S(2)}) collective-permute-start(bf16[208,2048]{1,0:T(8,128)(2,1)} %fusion.87), channel_id=1, source_target_pairs={{0,8},{4,12},{8,0},{12,4},{1,9},{5,13},{9,1},{13,5},{2,10},{6,14},... | collective-permute-start | bytes 2555912 | tf_op jit(solution)/shard_map/ppermute | solution.py:29
  114.6 3.1 %convolution_select_fusion.3 = f32[832,512]{1,0:T(8,128)} fusion(pred[832,512]{1,0:T(32,128)(4,1)S(1)} %copy-done.17, bf16[832,2048]{1,0:T(8,128)(2,1)S(1)} %pad_maximum_fusion.6, bf16[512,2048]{1,0:T(8,128)(2,1)S(1)} %bitcast.147), kind=kOutput, calls=%fused_computation.135 | convolution fusion | flops 1745256448 | bytes 7634944 | tf_op jit(solution)/shard_map/dot_general | solution.py:12
  117.7 2.7 %copy.25 = f32[832,512]{0,1:T(8,128)} copy(f32[832,512]{1,0:T(8,128)} %convolution_select_fusion.3) | data formatting | bytes 3407872 | tf_op jit(solution)/shard_map/jit(_where)/select_n | solution.py:64
  120.4 1.6 reduce_sum.47
  122.1 13.1 %all-reduce.8 = bf16[832,64]{0,1:T(8,128)(2,1)S(1)} all-reduce(f32[832,64]{0,1:T(8,128)S(1)} %reduce_sum.47), channel_id=1, replica_groups=mesh['groups'=2,'dp'=4,'mp'=2,'sub'=2] {'mp','sub'}, use_global_device_ids=true, to_apply=%region_6.7 | all-reduce | flops 53248 | bytes 319488 | tf_op jit(solution)/shard_map/psum | solution.py:84
  135.2 1.0 tile.18
  136.2 2.2 %copy.26 = bf16[832,512]{1,0:T(8,128)(2,1)} copy(bf16[832,512]{0,1:T(8,128)(2,1)} %bitcast.158) | data formatting | bytes 1703936 | tf_op jit(solution)/shard_map/tile | solution.py:67
  138.4 1.8 fusion.97
  140.2 6.4 %convolution_multiply_fusion.7 = f32[512,2048]{1,0:T(8,128)} fusion(bf16[832,512]{1,0:T(8,128)(2,1)S(1)} %broadcast_select_fusion, bf16[832,2048]{1,0:T(8,128)(2,1)} %copy-done.6), kind=kOutput, calls=%fused_computation.116 | convolution fusion | flops 1745879040 | bytes 8454144 | tf_op jit(solution)/shard_map/dot_general | solution.py:12
  146.7 0.8 pad_maximum_fusion.8
  147.5 43.9 %pmax.6 = s32[]{:T(128)} all-reduce(s32[]{:T(128)} %get-tuple-element.110), channel_id=1, replica_groups=mesh['groups'=2,'dp'=4,'mp'=2,'sub'=2] {'groups','dp'}, use_global_device_ids=true, to_apply=%region_8.9 | all-reduce | flops 1 | bytes 8 | tf_op jit(solution)/shard_map/pmax | solution.py:94
  191.4 2.7 %convolution_multiply_fusion.13 = f32[512,256]{1,0:T(8,128)} fusion(pred[832,512]{1,0:T(32,128)(4,1)} %copy-done.16, bf16[832,512]{1,0:T(8,128)(2,1)} %copy.26, bf16[208,256]{1,0:T(8,128)(2,1)S(1)} %copy-done.21, bf16[208,256]{1,0:T(8,128)(2,1)S(1)} %copy-done.23, bf16[208,256]{1,0:T(8,128)(2,1)S(1)} %copy-done.25, bf16[208,256]{1,0:T(8,128)(2,1)S(1)} %get-tuple-element.160), kind=kOutput, calls=%fused_computation.140 | convolution fusion | flops 220364800 | bytes 2228224 | tf_op jit(solution)/shard_map/dot_general | solution.py:12
  194.7 4.1 %all-to-all-start.3 = ((bf16[4,208,256]{2,1,0:T(8,128)(2,1)}), bf16[4,208,256]{2,1,0:T(8,128)(2,1)}, u32[]{:S(2)}, u32[]{:S(2)}) async-start(bf16[4,208,256]{2,1,0:T(8,128)(2,1)} %pad_maximum_fusion.8), calls=%async_computation.5 | async-start | bytes 851968 | tf_op jit(solution)/shard_map/all_to_all | solution.py:32
  198.8 0.8 fusion.137
  199.6 1.9 fusion.129
  201.5 2.1 fusion.126
  204.0 3.8 %add_convert_fusion.1 = bf16[512,2048]{1,0:T(8,128)(2,1)} fusion(f32[512,2048]{1,0:T(8,128)S(1)} %fusion.137, f32[512,2048]{1,0:T(8,128)S(1)} %fusion.129, f32[512,2048]{1,0:T(8,128)S(1)} %copy-done.7, f32[512,2048]{1,0:T(8,128)S(1)} %fusion.126, bf16[208,2048]{1,0:T(8,128)(2,1)} %collective-permute-done.11, s32[512]{0:T(512)S(1)} %fusion.172, ...), kind=kOutput, calls=%fused_computation.114 | convolution fusion | flops 441663488 | bytes 19728896 | tf_op jit(solution)/shard_map/dot_general | solution.py:12
  207.8 1.3 all-to-all-done.3
  209.0 1.8 fusion.104
  (72 shorter events, 5.1 us)
Async XLA Ops:
  7.2 61.4 %all-gather.5.cloned.1.call-start = ((), (), s32[]{:S(2)}) async-start(), calls=%async_computation.8 | async-start | bytes 1310720 | tf_op jit(solution)/shard_map/all_gather | solution.py:24
  11.7 9.3 %copy-start = (bf16[512,2048]{1,0:T(8,128)(2,1)S(1)}, bf16[512,2048]{1,0:T(8,128)(2,1)}, u32[]{:S(2)}) copy-start(bf16[512,2048]{1,0:T(8,128)(2,1)} %param.8) | copy-start | bytes 6291460
  14.7 19.4 %all-to-all-start.2 = ((bf16[4,224,256]{2,1,0:T(8,128)(2,1)}), bf16[4,224,256]{2,1,0:T(8,128)(2,1)S(1)}, u32[]{:S(2)}, u32[]{:S(2)}) async-start(bf16[4,224,256]{2,1,0:T(8,128)(2,1)} %fusion.119), calls=%async_computation.3 | async-start | bytes 917504 | tf_op jit(solution)/shard_map/all_to_all | solution.py:32
  21.0 188.0 %reduce-scatter.5.cloned.1.call-start = ((), (), s32[]{:S(2)}) async-start(), calls=%async_computation.9 | async-start | bytes 2621440 | tf_op jit(solution)/shard_map/reduce_scatter | solution.py:79
  34.1 4.6 %copy-start.20 = (bf16[208,256]{1,0:T(8,128)(2,1)}, bf16[208,256]{1,0:T(8,128)(2,1)S(1)}, u32[]{:S(2)}) copy-start(bf16[208,256]{1,0:T(8,128)(2,1)S(1)} %get-tuple-element.161) | copy-start | bytes 319492
  34.1 4.6 %copy-start.22 = (bf16[208,256]{1,0:T(8,128)(2,1)}, bf16[208,256]{1,0:T(8,128)(2,1)S(1)}, u32[]{:S(2)}) copy-start(bf16[208,256]{1,0:T(8,128)(2,1)S(1)} %get-tuple-element.162) | copy-start | bytes 319492
  34.2 4.6 %copy-start.24 = (bf16[208,256]{1,0:T(8,128)(2,1)}, bf16[208,256]{1,0:T(8,128)(2,1)S(1)}, u32[]{:S(2)}) copy-start(bf16[208,256]{1,0:T(8,128)(2,1)S(1)} %get-tuple-element.163) | copy-start | bytes 319492
  34.2 5.3 %copy-start.37 = (bf16[8,64,256]{2,1,0:T(8,128)(2,1)S(1)}, bf16[8,64,256]{2,1,0:T(8,128)(2,1)}, u32[]{:S(2)}) copy-start(bf16[8,64,256]{2,1,0:T(8,128)(2,1)} %param.11) | copy-start | bytes 786436
  34.3 45.0 %collective-permute-start.6 = (bf16[208,2048]{1,0:T(8,128)(2,1)}, bf16[208,2048]{1,0:T(8,128)(2,1)}, u32[]{:S(2)}, u32[]{:S(2)}) collective-permute-start(bf16[208,2048]{1,0:T(8,128)(2,1)} %convolution_convert_fusion.7), channel_id=1, source_target_pairs={{0,4},{4,8},{8,12},{12,0},{1,5},{5,9},{9,13},{13,1},{2,6},{6,10},{... | collective-permute-start | bytes 2555912 | tf_op jit(solution)/shard_map/ppermute | solution.py:29
  34.3 58.7 %collective-permute-start.7 = (bf16[208,2048]{1,0:T(8,128)(2,1)}, bf16[208,2048]{1,0:T(8,128)(2,1)}, u32[]{:S(2)}, u32[]{:S(2)}) collective-permute-start(bf16[208,2048]{1,0:T(8,128)(2,1)} %convolution_convert_fusion.6), channel_id=1, source_target_pairs={{0,8},{4,12},{8,0},{12,4},{1,9},{5,13},{9,1},{13,5},{2,10},{6,14},... | collective-permute-start | bytes 2555912 | tf_op jit(solution)/shard_map/ppermute | solution.py:29
  36.4 56.7 %collective-permute-start.8 = (bf16[208,2048]{1,0:T(8,128)(2,1)}, bf16[208,2048]{1,0:T(8,128)(2,1)}, u32[]{:S(2)}, u32[]{:S(2)}) collective-permute-start(bf16[208,2048]{1,0:T(8,128)(2,1)} %convolution_convert_fusion.5), channel_id=1, source_target_pairs={{0,12},{4,0},{8,4},{12,8},{1,13},{5,1},{9,5},{13,9},{2,14},{6,2},{... | collective-permute-start | bytes 2555912 | tf_op jit(solution)/shard_map/ppermute | solution.py:29
  38.7 0.8 copy-start.16
  60.4 2.0 copy-start.1
  68.5 7.0 %copy-start.35 = (bf16[2048,1024]{1,0:T(8,128)(2,1)S(1)}, bf16[2048,1024]{1,0:T(8,128)(2,1)}, u32[]{:S(2)}) copy-start(bf16[2048,1024]{1,0:T(8,128)(2,1)} %param.9) | copy-start | bytes 12582916
  79.3 35.3 %copy-start.2 = (bf16[8,2048,64]{1,2,0:T(8,128)(2,1)S(1)}, bf16[8,2048,64]{1,2,0:T(8,128)(2,1)}, u32[]{:S(2)}) copy-start(bf16[8,2048,64]{1,2,0:T(8,128)(2,1)} %param.10) | copy-start | bytes 6291460
  79.3 35.3 %copy-start.17 = (pred[832,512]{1,0:T(32,128)(4,1)S(1)}, pred[832,512]{1,0:T(32,128)(4,1)}, u32[]{:S(2)}) copy-start(pred[832,512]{1,0:T(32,128)(4,1)} %copy-done.16) | copy-start | bytes 1277956
  95.2 19.4 %copy-start.6 = (bf16[832,2048]{1,0:T(8,128)(2,1)}, bf16[832,2048]{1,0:T(8,128)(2,1)S(1)}, u32[]{:S(2)}) copy-start(bf16[832,2048]{1,0:T(8,128)(2,1)S(1)} %pad_maximum_fusion.6) | copy-start | bytes 10223620
  95.2 106.3 %collective-permute-start.9 = (bf16[208,2048]{1,0:T(8,128)(2,1)}, bf16[208,2048]{1,0:T(8,128)(2,1)}, u32[]{:S(2)}, u32[]{:S(2)}) collective-permute-start(bf16[208,2048]{1,0:T(8,128)(2,1)} %fusion.86), channel_id=1, source_target_pairs={{0,12},{4,0},{8,4},{12,8},{1,13},{5,1},{9,5},{13,9},{2,14},{6,2},{... | collective-permute-start | bytes 2555912 | tf_op jit(solution)/shard_map/ppermute | solution.py:29
  111.9 87.7 %collective-permute-start.10 = (bf16[208,2048]{1,0:T(8,128)(2,1)}, bf16[208,2048]{1,0:T(8,128)(2,1)}, u32[]{:S(2)}, u32[]{:S(2)}) collective-permute-start(bf16[208,2048]{1,0:T(8,128)(2,1)} %fusion.87), channel_id=1, source_target_pairs={{0,8},{4,12},{8,0},{12,4},{1,9},{5,13},{9,1},{13,5},{2,10},{6,14},... | collective-permute-start | bytes 2555912 | tf_op jit(solution)/shard_map/ppermute | solution.py:29
  114.6 89.1 %collective-permute-start.11 = (bf16[208,2048]{1,0:T(8,128)(2,1)}, bf16[208,2048]{1,0:T(8,128)(2,1)}, u32[]{:S(2)}, u32[]{:S(2)}) collective-permute-start(bf16[208,2048]{1,0:T(8,128)(2,1)} %fusion.88), channel_id=1, source_target_pairs={{0,4},{4,8},{8,12},{12,0},{1,5},{5,9},{9,13},{13,1},{2,6},{6,10},{... | collective-permute-start | bytes 2555912 | tf_op jit(solution)/shard_map/ppermute | solution.py:29
  140.2 51.2 %copy-start.21 = (bf16[208,256]{1,0:T(8,128)(2,1)S(1)}, bf16[208,256]{1,0:T(8,128)(2,1)}, u32[]{:S(2)}) copy-start(bf16[208,256]{1,0:T(8,128)(2,1)} %copy-done.20) | copy-start | bytes 319492
  140.2 51.1 %copy-start.23 = (bf16[208,256]{1,0:T(8,128)(2,1)S(1)}, bf16[208,256]{1,0:T(8,128)(2,1)}, u32[]{:S(2)}) copy-start(bf16[208,256]{1,0:T(8,128)(2,1)} %copy-done.22) | copy-start | bytes 319492
  140.2 51.1 %copy-start.25 = (bf16[208,256]{1,0:T(8,128)(2,1)S(1)}, bf16[208,256]{1,0:T(8,128)(2,1)}, u32[]{:S(2)}) copy-start(bf16[208,256]{1,0:T(8,128)(2,1)} %copy-done.24) | copy-start | bytes 319492
  191.3 7.5 %copy-start.12 = (bf16[208,2048]{1,0:T(8,128)(2,1)S(1)}, bf16[208,2048]{1,0:T(8,128)(2,1)}, u32[]{:S(2)}) copy-start(bf16[208,2048]{1,0:T(8,128)(2,1)} %fusion.89) | copy-start | bytes 2555908
  194.7 14.4 %all-to-all-start.3 = ((bf16[4,208,256]{2,1,0:T(8,128)(2,1)}), bf16[4,208,256]{2,1,0:T(8,128)(2,1)}, u32[]{:S(2)}, u32[]{:S(2)}) async-start(bf16[4,208,256]{2,1,0:T(8,128)(2,1)} %pad_maximum_fusion.8), calls=%async_computation.5 | async-start | bytes 851968 | tf_op jit(solution)/shard_map/all_to_all | solution.py:32
  201.5 2.4 %copy-start.7 = (f32[512,2048]{1,0:T(8,128)S(1)}, f32[512,2048]{1,0:T(8,128)}, u32[]{:S(2)}) copy-start(f32[512,2048]{1,0:T(8,128)} %fusion.188) | copy-start | bytes 12582916
  203.6 7.3 %copy-start.28 = (s32[512,1]{0,1:T(1,128)S(1)}, s32[512,1]{0,1:T(1,128)}, u32[]{:S(2)}) copy-start(s32[512,1]{0,1:T(1,128)} %param.13) | copy-start | bytes 6148
  203.6 7.3 %copy-start.38 = (bf16[8,64,256]{2,1,0:T(8,128)(2,1)S(1)}, bf16[8,64,256]{2,1,0:T(8,128)(2,1)}, u32[]{:S(2)}) copy-start(bf16[8,64,256]{2,1,0:T(8,128)(2,1)} %param.11) | copy-start | bytes 786436
  211.2 0.7 copy-start.41
Sparse Core Ops, SparseCore 0:
  9.6 19.5 all-gather.4
  79.4 31.4 reduce-scatter.4
